TPU v7x, 32 devices: a whole 2x2x4 slice. The times are simulated.
32 devices in a mesh: ctx: 8 (over y, x, core), grp: 4 (over z).
Axes of the slice: x: 2, y: 2, z: 4, core: 2. Of those that a mesh axis runs over, the one named last changes fastest.
Arguments:
- signal: bfloat16 [4096, 4096], P('ctx', 'grp'), may hold values from -6 to 6
- gate: bfloat16 [4096, 4096], P('ctx', 'grp'), may hold values from -6 to 6
- filter_taps: bfloat16 [4096, 512], P('ctx', 'grp'), may hold values from -0.09375 to 0.09375
- skip_gain: float32 [4096], P('grp'), may hold values from -4 to 4
- out_cotangent: bfloat16 [4096, 4096], P('ctx', 'grp'), may hold values from -6 to 6
Outputs:
- output: bfloat16 [4096, 4096], P('ctx', 'grp')
- grad_gate: bfloat16 [4096, 4096], P('ctx', 'grp')
- grad_signal: bfloat16 [4096, 4096], P('ctx', 'grp')
- grad_filter: float32 [4096, 512], P('ctx', 'grp')
All inputs are finite; a program needn't handle non-finite values.
Results may differ from a plain program's by a relative error of at most 0.011.
Values may be sent and summed in bfloat16 or wider, within the bound.
A program may use at most 192 MiB of HBM per device.

v0:
```python
import math

import jax
import jax.numpy as jnp
from jax import lax
from jax.sharding import PartitionSpec as P

TWO_PI = 2.0 * math.pi


def phase_pair(first_index, second_index, length):
    products_mod = first_index[:, None] * second_index[None, :] % length
    angles = products_mod.astype(jnp.float32) * (TWO_PI / length)
    return (jnp.cos(angles), -jnp.sin(angles))


def build_tables(devices_count, block_length, table_type):
    first_length = 2 * devices_count
    cosine_first, sine_first = phase_pair(
        jnp.arange(first_length, dtype=jnp.int32),
        jnp.arange(devices_count, dtype=jnp.int32),
        first_length,
    )
    stacked_rows = jnp.concatenate([cosine_first, sine_first], axis=0).astype(table_type)
    paired_rows = jnp.stack([cosine_first, sine_first], axis=0).astype(table_type)
    cosine_rows, sine_rows = phase_pair(
        jnp.arange(block_length, dtype=jnp.int32),
        jnp.arange(block_length, dtype=jnp.int32),
        block_length,
    )
    return (stacked_rows, paired_rows, cosine_rows.astype(table_type), sine_rows.astype(table_type))


def rotate_forward(first_out, first_freq, within_block, padded):
    half_rows = first_out.shape[0] // 2
    real_part = first_out[:half_rows]
    imag_part = first_out[half_rows:]
    twiddle_real, twiddle_imag = phase_pair(first_freq, within_block, padded)
    twiddle_real = twiddle_real[:, :, None]
    twiddle_imag = twiddle_imag[:, :, None]
    return jnp.stack(
        [
            real_part * twiddle_real - imag_part * twiddle_imag,
            real_part * twiddle_imag + imag_part * twiddle_real,
        ]
    )


def second_forward(rotated, cosine_rows, sine_rows):
    with_cosine = jnp.einsum(
        "jb,pkbc->pkjc", cosine_rows, rotated, preferred_element_type=jnp.float32
    )
    with_sine = jnp.einsum("jb,pkbc->pkjc", sine_rows, rotated, preferred_element_type=jnp.float32)
    return jnp.stack([with_cosine[0] - with_sine[1], with_cosine[1] + with_sine[0]])


def inverse_front(spectra, cosine_rows, sine_rows, first_freq, padded, precise):
    precision = lax.Precision.HIGHEST if precise else None
    operand = spectra if precise else spectra.astype(jnp.bfloat16)
    with_cosine = jnp.einsum(
        "jb,pkjc->pkbc",
        cosine_rows,
        operand,
        preferred_element_type=jnp.float32,
        precision=precision,
    )
    with_sine = jnp.einsum(
        "jb,pkjc->pkbc", sine_rows, operand, preferred_element_type=jnp.float32, precision=precision
    )
    real_turned = with_cosine[0] + with_sine[1]
    imag_turned = with_cosine[1] - with_sine[0]
    twiddle_real, twiddle_imag = phase_pair(
        first_freq, jnp.arange(spectra.shape[2], dtype=jnp.int32), padded
    )
    twiddle_real = twiddle_real[:, :, None]
    twiddle_imag = twiddle_imag[:, :, None]
    rotated = jnp.stack(
        [
            real_turned * twiddle_real + imag_turned * twiddle_imag,
            imag_turned * twiddle_real - real_turned * twiddle_imag,
        ]
    )
    if precise:
        return rotated
    return rotated.astype(jnp.bfloat16)


def inverse_back(rotated, paired_rows, padded, precise):
    precision = lax.Precision.HIGHEST if precise else None
    rows_out = jnp.einsum(
        "pka,pkbc->abc",
        paired_rows,
        rotated,
        preferred_element_type=jnp.float32,
        precision=precision,
    )
    return rows_out * (1.0 / padded)


def spectral_products(spectra, filter_low, width):
    filter_wide = filter_low.astype(jnp.float32)
    filter_real = filter_wide[0]
    filter_imag = filter_wide[1]
    input_real = spectra[0, ..., :width]
    input_imag = spectra[1, ..., :width]
    grad_real = spectra[0, ..., width:]
    grad_imag = spectra[1, ..., width:]
    channel_terms = jnp.stack(
        [
            jnp.concatenate(
                [
                    input_real * filter_real - input_imag * filter_imag,
                    grad_real * filter_real + grad_imag * filter_imag,
                ],
                axis=-1,
            ),
            jnp.concatenate(
                [
                    input_real * filter_imag + input_imag * filter_real,
                    grad_imag * filter_real - grad_real * filter_imag,
                ],
                axis=-1,
            ),
        ]
    )
    filter_term = jnp.stack(
        [
            input_real * grad_real + input_imag * grad_imag,
            input_real * grad_imag - input_imag * grad_real,
        ]
    )
    return (channel_terms, filter_term)


def split_forward(values, tables, position):
    stacked_rows, paired_rows, cosine_rows, sine_rows = tables
    devices_count = lax.axis_size("ctx")
    block_length = values.shape[0]
    lane_count = block_length // devices_count
    padded = 2 * devices_count * block_length
    first_length = 2 * devices_count
    first_out = jnp.einsum(
        "ka,abc->kbc",
        stacked_rows,
        lax.all_to_all(values[None], "ctx", split_axis=1, concat_axis=0, tiled=True),
        preferred_element_type=jnp.float32,
    )
    within_block = position * lane_count + jnp.arange(lane_count, dtype=jnp.int32)
    rotated = rotate_forward(
        first_out, jnp.arange(first_length, dtype=jnp.int32), within_block, padded
    ).astype(jnp.bfloat16)
    return second_forward(
        lax.all_to_all(rotated, "ctx", split_axis=1, concat_axis=2, tiled=True),
        cosine_rows,
        sine_rows,
    )


def split_inverse(spectra, tables, position, precise):
    stacked_rows, paired_rows, cosine_rows, sine_rows = tables
    devices_count = lax.axis_size("ctx")
    freq_count = spectra.shape[1]
    padded = 2 * devices_count * spectra.shape[2]
    first_freq = position * freq_count + jnp.arange(freq_count, dtype=jnp.int32)
    rotated = inverse_front(spectra, cosine_rows, sine_rows, first_freq, padded, precise)
    if precise:
        last_rows_out = inverse_back(
            lax.all_to_all(
                rotated.astype(jnp.bfloat16), "ctx", split_axis=2, concat_axis=1, tiled=True
            ).astype(rotated.dtype),
            paired_rows,
            padded,
            True,
        )
        result = lax.all_to_all(
            last_rows_out.astype(jnp.bfloat16), "ctx", split_axis=0, concat_axis=1, tiled=True
        ).astype(last_rows_out.dtype)
    else:
        rows_out = inverse_back(
            lax.all_to_all(rotated, "ctx", split_axis=2, concat_axis=1, tiled=True),
            paired_rows,
            padded,
            False,
        )
        result = lax.all_to_all(
            rows_out.astype(jnp.bfloat16), "ctx", split_axis=0, concat_axis=1, tiled=True
        ).astype(rows_out.dtype)
    return result[0]


def per_device(signal, gate, filter_taps, skip_gain, out_cotangent):
    devices_count = lax.axis_size("ctx")
    group_count = lax.axis_size("grp")
    block_length = signal.shape[0]
    local_channels = signal.shape[1]
    filters = filter_taps.shape[1] * group_count
    repeats = local_channels // filters
    position = lax.axis_index("ctx")
    coarse_tables = build_tables(devices_count, block_length, jnp.bfloat16)
    exact_tables = build_tables(devices_count, block_length, jnp.float32)
    gated = (out_cotangent.astype(jnp.float32) * gate.astype(jnp.float32)).astype(jnp.bfloat16)
    gain_wide = skip_gain[None, :]
    all_filters = lax.all_gather(filter_taps, "grp", axis=1, tiled=True)
    filter_low = lax.optimization_barrier(
        split_forward(all_filters, coarse_tables, position).astype(jnp.bfloat16)
    )
    filter_totals = jnp.zeros((2, 2, block_length, filters), jnp.float32)
    conv_blocks = []
    grad_blocks = []
    for block_index in range(repeats):
        lower = block_index * filters
        columns = jnp.concatenate(
            [signal[:, lower : lower + filters], gated[:, lower : lower + filters]], axis=1
        )
        spectra = split_forward(columns, coarse_tables, position)
        channel_terms, filter_term = spectral_products(spectra, filter_low, filters)
        filter_totals = filter_totals + filter_term
        signal_back = split_inverse(channel_terms, coarse_tables, position, False)
        conv_blocks.append(signal_back[:, :filters])
        grad_blocks.append(signal_back[:, filters:])
    conv_part = jnp.concatenate(conv_blocks, axis=1)
    grad_conv = jnp.concatenate(grad_blocks, axis=1)
    filter_back = split_inverse(filter_totals, exact_tables, position, True)
    grad_filter = lax.psum_scatter(
        filter_back.astype(jnp.bfloat16), "grp", scatter_dimension=1, tiled=True
    ).astype(jnp.float32)
    conv_part = conv_part + gain_wide * signal.astype(jnp.float32)
    output = (gate.astype(jnp.float32) * conv_part).astype(jnp.bfloat16)
    grad_gate = (out_cotangent.astype(jnp.float32) * conv_part).astype(jnp.bfloat16)
    grad_signal = (grad_conv + gain_wide * gated.astype(jnp.float32)).astype(jnp.bfloat16)
    scale = 1.0 / math.sqrt(devices_count * block_length * local_channels * group_count / filters)
    return (output, grad_gate, grad_signal, grad_filter * scale)


def solution(mesh):
    placed = (P("ctx", "grp"), P("ctx", "grp"), P("ctx", "grp"), P("grp"), P("ctx", "grp"))
    return jax.shard_map(
        per_device,
        mesh=mesh,
        in_specs=placed,
        out_specs=(P("ctx", "grp"), P("ctx", "grp"), P("ctx", "grp"), P("ctx", "grp")),
        check_vma=False,
    )
```

profile of v0, /device:TPU:0, one launch (start us, length us, event | category | flops | bytes accessed | tf_op | source)
XLA Modules:
  0.0 563.1 jit_solution(4340059187237713775)
XLA Ops:
  7.2 16.9 %all_gather.3 = bf16[512,512]{1,0:T(8,128)(2,1)S(1)} all-gather(bf16[512,128]{1,0:T(8,128)(2,1)} %param.7), channel_id=1, replica_groups=mesh['ctx'=8,'grp'=4] {'grp'}, dimensions={1}, use_global_device_ids=true | all-gather | bytes 655360 | tf_op jit(solution)/shard_map/all_gather | solution.py:203
  40.9 6.8 %reduce.2 = bf16[512,1024]{1,0:T(8,128)(2,1)S(1)} reduce(bf16[512,1,1024]{2,1,0:T(2,128)(2,1)S(1)} %bitcast.191, bf16[]{:T(256)} %broadcast.389), dimensions={1}, to_apply=%bitcast.183.reduce_sub_computation | reduce | bytes 2097154
  56.6 7.8 %reduce.1 = bf16[512,1024]{1,0:T(8,128)(2,1)} reduce(bf16[512,1,1024]{2,1,0:T(2,128)(2,1)S(1)} %bitcast.190, bf16[]{:T(256)} %broadcast.389), dimensions={1}, to_apply=%bitcast.184.reduce_sub_computation | reduce | bytes 2097154
  81.8 7.4 %all-to-all-done = bf16[8,2,32768]{2,1,0:T(2,128)(2,1)} async-done(((bf16[8,2,32768]{2,1,0:T(2,128)(2,1)}), bf16[8,2,32768]{2,1,0:T(2,128)(2,1)}, u32[]{:S(2)}, u32[]{:S(2)}) %all-to-all-start) | async-done | bytes 1048608 | tf_op jit(solution)/shard_map/all_to_all | solution.py:145
  110.4 9.8 %all-to-all-done.3 = bf16[2,16,64,512]{3,2,0,1:T(8,128)(2,1)} async-done(((bf16[2,16,64,512]{3,2,0,1:T(8,128)(2,1)}), bf16[2,16,64,512]{3,2,0,1:T(8,128)(2,1)}, u32[]{:S(2)}, u32[]{:S(2)}) %all-to-all-start.3) | async-done | bytes 2097184 | tf_op jit(solution)/shard_map/all_to_all | solution.py:153
  120.3 4.7 all-to-all-start.7
  131.3 42.8 %all-to-all-done.7 = bf16[2,16,64,1024]{3,2,0,1:T(8,128)(2,1)} async-done(((bf16[2,16,64,1024]{3,2,0,1:T(8,128)(2,1)}), bf16[2,16,64,1024]{3,2,0,1:T(8,128)(2,1)}, u32[]{:S(2)}, u32[]{:S(2)}) %all-to-all-start.7) | async-done | bytes 4194336 | tf_op jit(solution)/shard_map/all_to_all | solution.py:153
  180.8 8.2 %convolution_bitcast_fusion.9 = f32[2,2,512,512]{2,3,1,0:T(8,128)S(1)} fusion(bf16[2,2,512,512]{3,2,1,0:T(8,128)(2,1)S(1)} %bitcast.202), kind=kOutput, calls=%fused_computation.35 | convolution fusion | flops 1077673984 | bytes 6291456 | tf_op jit(solution)/shard_map/jb,pkbc->pkjc/dot_general | solution.py:50
  189.0 8.3 %convolution_bitcast_fusion.8 = f32[2,2,512,512]{2,3,1,0:T(8,128)S(1)} fusion(bf16[2,2,512,512]{3,2,1,0:T(8,128)(2,1)S(1)} %bitcast.203), kind=kOutput, calls=%fused_computation.34 | convolution fusion | flops 1077936128 | bytes 6291456 | tf_op jit(solution)/shard_map/jb,pkbc->pkjc/dot_general | solution.py:53
  204.0 9.0 %convolution_bitcast_fusion.3 = f32[2,2,512,1024]{2,3,1,0:T(8,128)} fusion(bf16[2,2,512,1024]{3,2,1,0:T(8,128)(2,1)S(1)} %bitcast.196), kind=kOutput, calls=%fused_computation.26 | convolution fusion | flops 2151415808 | bytes 12582912 | tf_op jit(solution)/shard_map/jb,pkbc->pkjc/dot_general | solution.py:50
  213.0 8.6 %convolution_bitcast_fusion.2 = f32[2,2,512,1024]{2,3,1,0:T(8,128)} fusion(bf16[2,2,512,1024]{3,2,1,0:T(8,128)(2,1)S(1)} %bitcast.197), kind=kOutput, calls=%fused_computation.25 | convolution fusion | flops 2151677952 | bytes 12582912 | tf_op jit(solution)/shard_map/jb,pkbc->pkjc/dot_general | solution.py:53
  221.6 6.3 %all-to-all-done.1 = bf16[2,16,64,1024]{3,2,0,1:T(8,128)(2,1)} async-done(((bf16[2,16,64,1024]{3,2,0,1:T(8,128)(2,1)}), bf16[2,16,64,1024]{3,2,0,1:T(8,128)(2,1)}, u32[]{:S(2)}, u32[]{:S(2)}) %all-to-all-start.1) | async-done | bytes 4194336 | tf_op jit(solution)/shard_map/all_to_all | solution.py:153
  230.5 8.6 %convolution_bitcast_fusion.6 = f32[2,2,512,1024]{2,3,1,0:T(8,128)} fusion(bf16[2,2,512,1024]{3,2,1,0:T(8,128)(2,1)S(1)} %bitcast.198), kind=kOutput, calls=%fused_computation.29 | convolution fusion | flops 2151677952 | bytes 12582912 | tf_op jit(solution)/shard_map/jb,pkbc->pkjc/dot_general | solution.py:53
  239.1 8.6 %convolution_bitcast_fusion.7 = f32[2,2,512,1024]{2,3,1,0:T(8,128)} fusion(bf16[2,2,512,1024]{3,2,1,0:T(8,128)(2,1)S(1)} %bitcast.199), kind=kOutput, calls=%fused_computation.30 | convolution fusion | flops 2151415808 | bytes 12582912 | tf_op jit(solution)/shard_map/jb,pkbc->pkjc/dot_general | solution.py:50
  247.7 9.9 %slice_add_fusion.1 = (f32[1,2,512,1024]{2,3,1,0:T(8,128)S(1)}, f32[1,2,512,1024]{2,3,1,0:T(8,128)}) fusion(f32[2,2,512,1024]{2,3,1,0:T(8,128)} %convolution_bitcast_fusion.2, f32[2,2,512,1024]{2,3,1,0:T(8,128)} %convolution_bitcast_fusion.3), kind=kLoop, calls=%fused_computation.2 | loop fusion | flops 2097152 | bytes 25165824 | tf_op jit(solution)/shard_map/add | solution.py:54
  262.2 11.3 %slice_add_fusion.3 = (f32[1,2,512,1024]{2,3,1,0:T(8,128)}, f32[1,2,512,1024]{2,3,1,0:T(8,128)}) fusion(f32[2,2,512,1024]{2,3,1,0:T(8,128)} %convolution_bitcast_fusion.6, f32[2,2,512,1024]{2,3,1,0:T(8,128)} %convolution_bitcast_fusion.7), kind=kLoop, calls=%fused_computation.6 | loop fusion | flops 2097152 | bytes 25165824 | tf_op jit(solution)/shard_map/add | solution.py:54
  278.1 10.9 %convolution_bitcast_fusion.11 = f32[2,2,512,512]{2,3,1,0:T(8,128)S(1)} fusion(f32[1,2,512,512]{2,3,1,0:T(8,128)S(1)} %get-tuple-element.29, f32[1,2,512,512]{2,3,1,0:T(8,128)S(1)} %get-tuple-element.28, f32[1,2,512,512]{2,3,1,0:T(8,128)S(1)} %copy-done.18, f32[1,2,512,512]{2,3,1,0:T(8,128)S(1)} %get-tuple-element.26), kind=kOutput, calls=%fused_computation.37 | convolution fusion | flops 6449266688 | bytes 12582912 | tf_op jit(solution)/shard_map/jb,pkjc->pkbc/dot_general | solution.py:60
  289.0 11.2 %convolution_bitcast_fusion.10 = f32[2,2,512,512]{2,3,1,0:T(8,128)S(1)} fusion(f32[1,2,512,512]{2,3,1,0:T(8,128)S(1)} %get-tuple-element.29, f32[1,2,512,512]{2,3,1,0:T(8,128)S(1)} %get-tuple-element.28, f32[1,2,512,512]{2,3,1,0:T(8,128)S(1)} %copy-done.18, f32[1,2,512,512]{2,3,1,0:T(8,128)S(1)} %get-tuple-element.26), kind=kOutput, calls=%fused_computation.36 | convolution fusion | flops 6449528832 | bytes 12582912 | tf_op jit(solution)/shard_map/jb,pkjc->pkbc/dot_general | solution.py:67
  322.9 8.8 %convolution_bitcast_fusion.1 = f32[2,2,512,1024]{2,3,1,0:T(8,128)} fusion(bf16[1,2,512,1024]{2,3,1,0:T(8,128)(2,1)S(1)} %maximum_bitcast_fusion.3, bf16[1,2,512,1024]{2,3,1,0:T(8,128)(2,1)S(1)} %maximum_bitcast_fusion.2), kind=kOutput, calls=%fused_computation.24 | convolution fusion | flops 2153512960 | bytes 12582912 | tf_op jit(solution)/shard_map/jb,pkjc->pkbc/dot_general | solution.py:60
  331.6 8.8 %convolution_bitcast_fusion.5 = f32[2,2,512,1024]{2,3,1,0:T(8,128)} fusion(bf16[1,2,512,1024]{2,3,1,0:T(8,128)(2,1)S(1)} %maximum_bitcast_fusion.1, bf16[1,2,512,1024]{2,3,1,0:T(8,128)(2,1)S(1)} %maximum_bitcast_fusion), kind=kOutput, calls=%fused_computation.28 | convolution fusion | flops 2153512960 | bytes 12582912 | tf_op jit(solution)/shard_map/jb,pkjc->pkbc/dot_general | solution.py:60
  340.4 9.1 %convolution_bitcast_fusion = f32[2,2,512,1024]{2,3,1,0:T(8,128)} fusion(bf16[1,2,512,1024]{2,3,1,0:T(8,128)(2,1)S(1)} %maximum_bitcast_fusion.3, bf16[1,2,512,1024]{2,3,1,0:T(8,128)(2,1)S(1)} %maximum_bitcast_fusion.2), kind=kOutput, calls=%fused_computation.23 | convolution fusion | flops 2153775104 | bytes 12582912 | tf_op jit(solution)/shard_map/jb,pkjc->pkbc/dot_general | solution.py:67
  349.5 8.9 %convolution_bitcast_fusion.4 = f32[2,2,512,1024]{2,3,1,0:T(8,128)} fusion(bf16[1,2,512,1024]{2,3,1,0:T(8,128)(2,1)S(1)} %maximum_bitcast_fusion.1, bf16[1,2,512,1024]{2,3,1,0:T(8,128)(2,1)S(1)} %maximum_bitcast_fusion), kind=kOutput, calls=%fused_computation.27 | convolution fusion | flops 2153775104 | bytes 12582912 | tf_op jit(solution)/shard_map/jb,pkjc->pkbc/dot_general | solution.py:67
  371.6 13.4 %add_convert_fusion.2 = (bf16[1,2,512,1024]{2,3,1,0:T(8,128)(2,1)S(1)}, bf16[1,2,512,1024]{2,3,1,0:T(8,128)(2,1)S(1)}, bf16[1,2,512,1024]{2,3,1,0:T(8,128)(2,1)S(1)}, bf16[1,2,512,1024]{2,3,1,0:T(8,128)(2,1)}) fusion(f32[2,512]{1,0:T(2,128)S(1)} %get-tuple-element.52, f32[2,512]{1,0:T(2,128)S(1)} %get-tuple-element.51, ...), kind=kLoop, calls=%fused_computation.20 | loop fusion | flops 20971520 | bytes 41951232 | tf_op jit(solution)/shard_map/convert.22
  387.4 11.3 %copy.76 = bf16[2,2,512,1024]{3,1,0,2:T(2,128)(2,1)} copy(bf16[2,2,512,1024]{2,3,1,0:T(8,128)(2,1)} %pad_maximum_fusion.2) | data formatting | bytes 8388608 | tf_op jit(solution)/shard_map/stack | solution.py:77
  407.2 11.4 %copy.87 = bf16[2,2,512,1024]{3,1,0,2:T(2,128)(2,1)} copy(bf16[2,2,512,1024]{2,3,1,0:T(8,128)(2,1)} %pad_maximum_fusion.5) | data formatting | bytes 8388608 | tf_op jit(solution)/shard_map/stack | solution.py:77
  418.6 33.9 %all-to-all-done.4 = bf16[2,2,512,1024]{3,1,0,2:T(2,128)(2,1)} async-done(((bf16[2,2,512,1024]{3,1,0,2:T(2,128)(2,1)}), bf16[2,2,512,1024]{3,1,0,2:T(2,128)(2,1)}, u32[]{:S(2)}, u32[]{:S(2)}) %all-to-all-start.4) | async-done | bytes 4194336 | tf_op jit(solution)/shard_map/all_to_all | solution.py:180
  461.7 6.4 %copy.78 = bf16[2,8,2,64,1024]{4,2,1,0,3:T(2,128)(2,1)} copy(bf16[2,8,2,64,1024]{4,3,1,2,0:T(8,128)(2,1)S(1)} %bitcast.186) | data formatting | bytes 8388608 | tf_op jit(solution)/shard_map/all_to_all | solution.py:180
  468.0 7.4 %all_to_all.143 = bf16[2,16,64,1024]{3,1,0,2:T(8,128)(2,1)} reshape(bf16[2,8,2,64,1024]{4,2,1,0,3:T(2,128)(2,1)} %copy.78) | data formatting | bytes 8388608 | tf_op jit(solution)/shard_map/all_to_all | solution.py:180
  479.9 26.2 %all-to-all-done.8 = bf16[2,2,512,1024]{3,1,0,2:T(2,128)(2,1)} async-done(((bf16[2,2,512,1024]{3,1,0,2:T(2,128)(2,1)}), bf16[2,2,512,1024]{3,1,0,2:T(2,128)(2,1)}, u32[]{:S(2)}, u32[]{:S(2)}) %all-to-all-start.8) | async-done | bytes 4194336 | tf_op jit(solution)/shard_map/all_to_all | solution.py:180
  513.3 6.3 %copy.89 = bf16[2,8,2,64,1024]{4,2,1,0,3:T(2,128)(2,1)} copy(bf16[2,8,2,64,1024]{4,3,1,2,0:T(8,128)(2,1)S(1)} %bitcast.187) | data formatting | bytes 8388608 | tf_op jit(solution)/shard_map/all_to_all | solution.py:180
  519.6 7.3 %all_to_all.154 = bf16[2,16,64,1024]{3,1,0,2:T(8,128)(2,1)} reshape(bf16[2,8,2,64,1024]{4,2,1,0,3:T(2,128)(2,1)} %copy.89) | data formatting | bytes 8388608 | tf_op jit(solution)/shard_map/all_to_all | solution.py:180
  538.8 12.1 %all-to-all-done.9 = bf16[8,64,1024]{2,1,0:T(8,128)(2,1)S(1)} async-done(((bf16[8,64,1024]{2,1,0:T(8,128)(2,1)}), bf16[8,64,1024]{2,1,0:T(8,128)(2,1)S(1)}, u32[]{:S(2)}, u32[]{:S(2)}) %all-to-all-start.9) | async-done | bytes 1048608 | tf_op jit(solution)/shard_map/all_to_all | solution.py:185
  (132 shorter events, 179.9 us)
Async XLA Ops:
  24.9 11.8 %copy-start.11 = (bf16[512,1024]{1,0:T(8,128)(2,1)S(1)}, bf16[512,1024]{1,0:T(8,128)(2,1)}, u32[]{:S(2)}) copy-start(bf16[512,1024]{1,0:T(8,128)(2,1)} %param.9) | copy-start | bytes 3145732
  24.9 11.8 %copy-start.13 = (bf16[512,1024]{1,0:T(8,128)(2,1)S(1)}, bf16[512,1024]{1,0:T(8,128)(2,1)}, u32[]{:S(2)}) copy-start(bf16[512,1024]{1,0:T(8,128)(2,1)} %param.6) | copy-start | bytes 3145732
  32.3 16.9 %all-to-all-start.2 = ((bf16[8,2,16384]{2,1,0:T(2,128)(2,1)}), bf16[8,2,16384]{2,1,0:T(2,128)(2,1)}, u32[]{:S(2)}, u32[]{:S(2)}) async-start(bf16[8,2,16384]{2,1,0:T(2,128)(2,1)} %reshape.274), calls=%async_computation.2 | async-start | bytes 1048576 | tf_op jit(solution)/shard_map/all_to_all | solution.py:145
  36.7 1.2 copy-start.15
  49.3 19.8 %all-to-all-start.6 = ((bf16[8,2,32768]{2,1,0:T(2,128)(2,1)}), bf16[8,2,32768]{2,1,0:T(2,128)(2,1)S(1)}, u32[]{:S(2)}, u32[]{:S(2)}) async-start(bf16[8,2,32768]{2,1,0:T(2,128)(2,1)} %reshape.276), calls=%async_computation.6 | async-start | bytes 2097152 | tf_op jit(solution)/shard_map/all_to_all | solution.py:145
  69.1 20.2 %all-to-all-start = ((bf16[8,2,32768]{2,1,0:T(2,128)(2,1)}), bf16[8,2,32768]{2,1,0:T(2,128)(2,1)}, u32[]{:S(2)}, u32[]{:S(2)}) async-start(bf16[8,2,32768]{2,1,0:T(2,128)(2,1)} %reshape.278), calls=%async_computation | async-start | bytes 2097152 | tf_op jit(solution)/shard_map/all_to_all | solution.py:145
  89.2 31.0 %all-to-all-start.3 = ((bf16[2,16,64,512]{3,2,0,1:T(8,128)(2,1)}), bf16[2,16,64,512]{3,2,0,1:T(8,128)(2,1)}, u32[]{:S(2)}, u32[]{:S(2)}) async-start(bf16[2,16,64,512]{3,2,0,1:T(8,128)(2,1)} %copy.71), calls=%async_computation.3 | async-start | bytes 4194304 | tf_op jit(solution)/shard_map/all_to_all | solution.py:153
  120.3 53.9 %all-to-all-start.7 = ((bf16[2,16,64,1024]{3,2,0,1:T(8,128)(2,1)}), bf16[2,16,64,1024]{3,2,0,1:T(8,128)(2,1)}, u32[]{:S(2)}, u32[]{:S(2)}) async-start(bf16[2,16,64,1024]{3,2,0,1:T(8,128)(2,1)} %copy.82), calls=%async_computation.7 | async-start | bytes 8388608 | tf_op jit(solution)/shard_map/all_to_all | solution.py:153
  174.1 53.7 %all-to-all-start.1 = ((bf16[2,16,64,1024]{3,2,0,1:T(8,128)(2,1)}), bf16[2,16,64,1024]{3,2,0,1:T(8,128)(2,1)}, u32[]{:S(2)}, u32[]{:S(2)}) async-start(bf16[2,16,64,1024]{3,2,0,1:T(8,128)(2,1)} %copy.64), calls=%async_computation.1 | async-start | bytes 8388608 | tf_op jit(solution)/shard_map/all_to_all | solution.py:153
  273.5 4.7 copy-start.18
  289.0 11.2 %copy-start = (f32[1,2,512,1024]{2,3,1,0:T(8,128)S(1)}, f32[1,2,512,1024]{2,3,1,0:T(8,128)}, u32[]{:S(2)}) copy-start(f32[1,2,512,1024]{2,3,1,0:T(8,128)} %get-tuple-element.11) | copy-start | bytes 12582916
  289.0 11.2 %copy-start.3 = (f32[2,2,512,512]{2,3,1,0:T(8,128)S(1)}, f32[2,2,512,512]{2,3,1,0:T(8,128)}, u32[]{:S(2)}) copy-start(f32[2,2,512,512]{2,3,1,0:T(8,128)} %convert_element_type.182) | copy-start | bytes 12582916
  300.2 3.6 copy-start.1
  300.2 4.6 copy-start.2
  314.0 44.4 %all-to-all-start.10 = ((bf16[2,2,512,512]{3,1,0,2:T(2,128)(2,1)}), bf16[2,2,512,512]{3,1,0,2:T(2,128)(2,1)S(1)}, u32[]{:S(2)}, u32[]{:S(2)}) async-start(bf16[2,2,512,512]{3,1,0,2:T(2,128)(2,1)} %copy.91), calls=%async_computation.10 | async-start | bytes 4194304 | tf_op jit(solution)/shard_map/all_to_all | solution.py:168
  317.8 1.9 copy-start.6
  319.7 1.2 copy-start.9
  319.7 1.5 copy-start.10
  321.2 1.2 copy-start.7
  321.2 1.5 copy-start.8
  367.5 31.2 %all-to-all-start.11 = ((bf16[8,64,512]{2,1,0:T(8,128)(2,1)}), bf16[8,64,512]{2,1,0:T(8,128)(2,1)S(1)}, u32[]{:S(2)}, u32[]{:S(2)}) async-start(bf16[8,64,512]{2,1,0:T(8,128)(2,1)} %copy.94), calls=%async_computation.11 | async-start | bytes 1048576 | tf_op jit(solution)/shard_map/all_to_all | solution.py:175
  398.7 53.7 %all-to-all-start.4 = ((bf16[2,2,512,1024]{3,1,0,2:T(2,128)(2,1)}), bf16[2,2,512,1024]{3,1,0,2:T(2,128)(2,1)}, u32[]{:S(2)}, u32[]{:S(2)}) async-start(bf16[2,2,512,1024]{3,1,0,2:T(2,128)(2,1)} %copy.76), calls=%async_computation.4 | async-start | bytes 8388608 | tf_op jit(solution)/shard_map/all_to_all | solution.py:180
  452.5 53.7 %all-to-all-start.8 = ((bf16[2,2,512,1024]{3,1,0,2:T(2,128)(2,1)}), bf16[2,2,512,1024]{3,1,0,2:T(2,128)(2,1)}, u32[]{:S(2)}, u32[]{:S(2)}) async-start(bf16[2,2,512,1024]{3,1,0,2:T(2,128)(2,1)} %copy.87), calls=%async_computation.8 | async-start | bytes 8388608 | tf_op jit(solution)/shard_map/all_to_all | solution.py:180
  457.0 78.5 %reduce-scatter.4.cloned.1.call-start = ((), (), s32[]{:S(2)}) async-start(), calls=%async_computation.13 | async-start | bytes 655360
  506.1 25.2 %all-to-all-start.5 = ((bf16[8,64,1024]{2,1,0:T(8,128)(2,1)}), bf16[8,64,1024]{2,1,0:T(8,128)(2,1)S(1)}, u32[]{:S(2)}, u32[]{:S(2)}) async-start(bf16[8,64,1024]{2,1,0:T(8,128)(2,1)} %copy.79), calls=%async_computation.5 | async-start | bytes 2097152 | tf_op jit(solution)/shard_map/all_to_all | solution.py:185
  531.4 19.5 %all-to-all-start.9 = ((bf16[8,64,1024]{2,1,0:T(8,128)(2,1)}), bf16[8,64,1024]{2,1,0:T(8,128)(2,1)S(1)}, u32[]{:S(2)}, u32[]{:S(2)}) async-start(bf16[8,64,1024]{2,1,0:T(8,128)(2,1)} %copy.90), calls=%async_computation.9 | async-start | bytes 2097152 | tf_op jit(solution)/shard_map/all_to_all | solution.py:185
  550.9 1.2 copy-start.17
  551.2 1.3 copy-start.5
  551.2 1.6 copy-start.12
  551.2 1.9 copy-start.14
  551.3 2.2 copy-start.16
  551.3 2.2 copy-start.19
  (1 other events, 1.0 us)
Sparse Core Ops, SparseCore 0:
  460.7 21.9 reduce-scatter.3
where the time goes:
time: 570 us; the launch traced here: 563 us
  waiting for transfers between devices  141 us (25%)
  local copies, waits for them, and re-layouts  122 us (21%)
  matrix products  119 us (21%)
  other arithmetic  98.1 us (17%)
  starting transfers between devices  51.9 us (9%)
  blocking collectives  16.9 us (3%)
  between operations  14.8 us (3%)
    all_to_all x2, waiting for transfers between devices, split_inverse(): lax.all_to_all(rotated, 'ctx', split_axis=2, concat_axis=1, tiled=True)  60.1 us
    all_to_all x3, waiting for transfers between devices, split_forward(): lax.all_to_all(rotated, 'ctx', split_axis=1, concat_axis=2, tiled=True)  58.9 us
    all_to_all x6, local copies, waits for them, and re-layouts, split_inverse(): lax.all_to_all(rotated, 'ctx', split_axis=2, concat_axis=1, tiled=True)  34.5 us
    dot_general x3, matrix products, inverse_front(): jnp.einsum('jb,pkjc->pkbc', sine_rows, operand, preferred_element_type=jn...  29.2 us
    dot_general x3, matrix products, inverse_front(): jnp.einsum('jb,pkjc->pkbc', cosine_rows, operand, preferred_element_type=...  28.4 us
    another operation x3, local copies, waits for them, and re-layouts, inverse_front(): jnp.stack([real_turned * twiddle_real + imag_turned * twiddle_imag, imag_...  26.8 us
    dot_general x3, matrix products, second_forward(): jnp.einsum('jb,pkbc->pkjc', cosine_rows, rotated, preferred_element_type=...  25.8 us
    dot_general x3, matrix products, second_forward(): jnp.einsum('jb,pkbc->pkjc', sine_rows, rotated, preferred_element_type=jn...  25.5 us
  transfers between devices with their start and end apart: 13, of which 8 were waited for; matrix products, arithmetic and copies ran while one was open for 38% of the time, Pallas kernels for 0%

commit v1 on v0

--- a/solution.py
+++ b/solution.py
@@ -2,7 +2,11 @@
 
 import jax
 import jax.numpy as jnp
+import ml_dtypes
+import numpy as np
 from jax import lax
+from jax.experimental import pallas as pl
+from jax.experimental.pallas import tpu as pltpu
 from jax.sharding import PartitionSpec as P
 
 TWO_PI = 2.0 * math.pi
@@ -188,7 +192,7 @@
     return result[0]
 
 
-def per_device(signal, gate, filter_taps, skip_gain, out_cotangent):
+def per_device_general(signal, gate, filter_taps, skip_gain, out_cotangent):
     devices_count = lax.axis_size("ctx")
     group_count = lax.axis_size("grp")
     block_length = signal.shape[0]
@@ -232,6 +236,411 @@
     return (output, grad_gate, grad_signal, grad_filter * scale)
 
 
+CTX = 8
+FIRST = 16
+ROWS = 512
+LANES = 128
+HALF = 64
+STRIP = 16
+
+
+def low(values):
+    return np.asarray(values, np.float32).astype(ml_dtypes.bfloat16)
+
+
+def first_coefficients():
+    index = np.arange(FIRST)
+    angles = (index[:, None] * index[None, :] % FIRST).astype(np.float32) * np.float32(TWO_PI / FIRST)
+    return (
+        low(np.round(np.cos(angles), 7)).astype(np.float64),
+        low(np.round(np.sin(angles), 7)).astype(np.float64),
+    )
+
+
+def dense_tables():
+    index = np.arange(ROWS)
+    angles = (index[:, None] * index[None, :] % ROWS).astype(np.float32) * np.float32(TWO_PI / ROWS)
+    wide = low(np.cos(angles)).astype(np.float64) - 1j * low(np.sin(angles)).astype(np.float64)
+    freq = np.arange(FIRST)
+    padded = FIRST * ROWS
+    turn = np.exp(-2j * np.pi * (freq[:, None] * index[None, :] % padded) / padded)
+    both = wide[None] * turn[:, None, :]
+    forward = low(np.concatenate([both.real, both.imag], axis=2))
+    back = both.transpose(0, 2, 1) / padded
+    inverse = low(np.concatenate([back.real, -back.imag], axis=2))
+    return forward, inverse
+
+
+COS, SIN = first_coefficients()
+
+
+def scaled_sum(terms):
+    total = None
+    for coefficient, value in terms:
+        coefficient = float(coefficient)
+        if abs(coefficient) < 1e-6:
+            continue
+        if total is None:
+            total = value if coefficient == 1.0 else value * coefficient
+        elif coefficient == 1.0:
+            total = total + value
+        elif coefficient == -1.0:
+            total = total - value
+        else:
+            total = total + value * coefficient
+    return total
+
+
+def lower_half(shape):
+    return lax.broadcasted_iota(jnp.int32, shape, len(shape) - 1) < HALF
+
+
+def swap(values):
+    return pltpu.roll(values, HALF, axis=1)
+
+
+def times_i(values, sign):
+    return swap(values) * sign
+
+
+def forward_first(blocks, sign):
+    plus = {a: blocks[a] + blocks[8 - a] for a in (1, 2, 3)}
+    minus = {a: blocks[a] - blocks[8 - a] for a in (1, 2, 3)}
+    results = [None] * FIRST
+    for k in range(9):
+        if k % 2 == 0:
+            real = scaled_sum(
+                [(1.0, blocks[0]), (COS[k, 4], blocks[4])] + [(COS[k, a], plus[a]) for a in (1, 2, 3)]
+            )
+            turned = scaled_sum([(-SIN[k, a], minus[a]) for a in (1, 2, 3)])
+        else:
+            real = scaled_sum([(1.0, blocks[0])] + [(COS[k, a], minus[a]) for a in (1, 2, 3)])
+            turned = scaled_sum([(-SIN[k, 4], blocks[4])] + [(-SIN[k, a], plus[a]) for a in (1, 2, 3)])
+        if turned is None:
+            results[k] = real
+            continue
+        turned = times_i(turned, sign)
+        results[k] = real + turned
+        results[FIRST - k] = real - turned
+    return results
+
+
+def inverse_last(parts, sign):
+    even = {k: parts[k] + parts[FIRST - k] for k in range(1, 8)}
+    odd = {k: parts[k] - parts[FIRST - k] for k in range(1, 8)}
+    results = [None] * CTX
+    for a in range(5):
+        flip = 1.0 if a % 2 == 0 else -1.0
+        real_even = scaled_sum(
+            [(1.0, parts[0]), (flip, parts[8])] + [(COS[k, a], even[k]) for k in (2, 4, 6)]
+        )
+        real_odd = scaled_sum([(COS[k, a], even[k]) for k in (1, 3, 5, 7)])
+        turn_even = scaled_sum([(SIN[k, a], odd[k]) for k in (2, 4, 6)])
+        turn_odd = scaled_sum([(SIN[k, a], odd[k]) for k in (1, 3, 5, 7)])
+        real = real_even if real_odd is None else real_even + real_odd
+        if a == 0:
+            results[0] = real
+            continue
+        if a == 4:
+            results[4] = real + times_i(turn_odd, sign)
+            continue
+        results[a] = real + times_i(turn_even + turn_odd, sign)
+        results[8 - a] = (real_even - real_odd) + times_i(turn_odd - turn_even, sign)
+    return results
+
+
+def signs():
+    return jnp.where(lower_half((1, LANES)), -1.0, 1.0).astype(jnp.float32)
+
+
+def store_stacked(ref, k, rows, lanes, values, sign):
+    top = pl.ds(rows, values.shape[0])
+    bottom = pl.ds(ROWS + rows, values.shape[0])
+    ref[k, top, lanes] = values.astype(jnp.bfloat16)
+    ref[k, bottom, lanes] = times_i(values, sign).astype(jnp.bfloat16)
+
+
+def stage_one(load, stacked_ref, lane_start):
+    sign = signs()
+
+    @pl.loop(0, ROWS // STRIP)
+    def _(strip):
+        rows = pl.multiple_of(strip * STRIP, STRIP)
+        blocks = [load(a, pl.ds(rows, STRIP)) for a in range(CTX)]
+        for k, values in enumerate(forward_first(blocks, sign)):
+            store_stacked(
+                stacked_ref, k, rows, slice(lane_start, lane_start + LANES), values, sign
+            )
+
+
+def last_stage(half_ref, lane_start, store):
+    sign = signs()
+
+    @pl.loop(0, ROWS // STRIP)
+    def _(strip):
+        rows = pl.multiple_of(strip * STRIP, STRIP)
+        parts = [
+            half_ref[k, pl.ds(rows, STRIP), lane_start : lane_start + LANES].astype(jnp.float32)
+            for k in range(FIRST)
+        ]
+        for a, values in enumerate(inverse_last(parts, sign)):
+            store(a, pl.ds(rows, STRIP), values)
+
+
+def conv_kernel(signal_ref, taps_ref, forward_ref, inverse_ref, conv_ref, spec_ref, filt_ref,
+                stacked, half):
+    k = pl.program_id(0)
+
+    @pl.when(k == 0)
+    def _():
+        stage_one(lambda a, rows: signal_ref[a, rows, :].astype(jnp.float32), stacked, 0)
+
+        def load_taps(a, rows):
+            values = taps_ref[a, rows, :].astype(jnp.float32)
+            return jnp.concatenate([values, jnp.zeros_like(values)], axis=1)
+
+        stage_one(load_taps, stacked, LANES)
+
+    sign = signs()
+    spectra = jnp.dot(forward_ref[0], stacked[k], preferred_element_type=jnp.float32)
+    signal_spec = spectra[:, :LANES]
+    filter_low = spectra[:, LANES:].astype(jnp.bfloat16)
+    spec_ref[0] = signal_spec.astype(jnp.bfloat16)
+    filt_ref[0] = filter_low
+    filter_wide = filter_low.astype(jnp.float32)
+    swapped = swap(filter_wide)
+    first_half = lower_half((ROWS, LANES))
+    filter_real = jnp.where(first_half, filter_wide, swapped)
+    filter_imag = jnp.where(first_half, swapped, filter_wide)
+    product = signal_spec * filter_real + times_i(signal_spec, sign) * filter_imag
+    operand = jnp.concatenate([product, times_i(product, sign)], axis=0).astype(jnp.bfloat16)
+    half[k] = jnp.dot(inverse_ref[0], operand, preferred_element_type=jnp.float32).astype(
+        jnp.bfloat16
+    )
+
+    @pl.when(k == FIRST - 1)
+    def _():
+        def store(a, rows, values):
+            conv_ref[a, rows, :] = values.astype(jnp.bfloat16)
+
+        last_stage(half, 0, store)
+
+
+def grad_kernel(gated_ref, spec_ref, filt_ref, forward_ref, inverse_ref, grad_ref, taps_ref,
+                stacked, half):
+    k = pl.program_id(0)
+
+    @pl.when(k == 0)
+    def _():
+        stage_one(lambda a, rows: gated_ref[a, rows, :].astype(jnp.float32), stacked, 0)
+
+    sign = signs()
+    spectra = jnp.dot(forward_ref[0], stacked[k], preferred_element_type=jnp.float32)
+    turned = times_i(spectra, sign)
+    first_half = lower_half((ROWS, LANES))
+
+    def split(values):
+        swapped = swap(values)
+        return jnp.where(first_half, values, swapped), jnp.where(first_half, swapped, values)
+
+    filter_real, filter_imag = split(filt_ref[0].astype(jnp.float32))
+    signal_real, signal_imag = split(spec_ref[0].astype(jnp.float32))
+    back = spectra * filter_real - turned * filter_imag
+    cross = spectra * signal_real - turned * signal_imag
+    operand = jnp.concatenate(
+        [
+            jnp.concatenate([back, cross], axis=1),
+            jnp.concatenate([times_i(back, sign), times_i(cross, sign)], axis=1),
+        ],
+        axis=0,
+    ).astype(jnp.bfloat16)
+    half[k] = jnp.dot(inverse_ref[0], operand, preferred_element_type=jnp.float32).astype(
+        jnp.bfloat16
+    )
+
+    @pl.when(k == FIRST - 1)
+    def _():
+        def store(a, rows, values):
+            grad_ref[a, rows, :] = values.astype(jnp.bfloat16)
+
+        def store_taps(a, rows, values):
+            taps_ref[a, rows, :] = values[:, :HALF].astype(jnp.bfloat16)
+
+        last_stage(half, 0, store)
+        last_stage(half, LANES, store_taps)
+
+
+def whole_spec(shape):
+    return pl.BlockSpec(shape, lambda k: (0,) * len(shape))
+
+
+def each_spec(shape):
+    return pl.BlockSpec((1,) + shape, lambda k: (k,) + (0,) * len(shape))
+
+
+TABLE_SPEC = each_spec((ROWS, 2 * ROWS))
+PARAMS = pltpu.CompilerParams(vmem_limit_bytes=56 * 1024 * 1024)
+WORK = 2 * FIRST * ROWS * 2 * ROWS * 2 * LANES * 2
+COST = pl.CostEstimate(flops=WORK, bytes_accessed=40 * 1024 * 1024, transcendentals=0)
+
+
+def conv_call(signal_blocks, taps_blocks, forward, inverse):
+    block = (CTX, ROWS, LANES)
+    return pl.pallas_call(
+        conv_kernel,
+        grid=(FIRST,),
+        in_specs=[whole_spec(block), whole_spec((CTX, ROWS, HALF)), TABLE_SPEC, TABLE_SPEC],
+        out_specs=[whole_spec(block), each_spec((ROWS, LANES)), each_spec((ROWS, LANES))],
+        out_shape=[
+            jax.ShapeDtypeStruct(block, jnp.bfloat16),
+            jax.ShapeDtypeStruct((FIRST, ROWS, LANES), jnp.bfloat16),
+            jax.ShapeDtypeStruct((FIRST, ROWS, LANES), jnp.bfloat16),
+        ],
+        scratch_shapes=[
+            pltpu.VMEM((FIRST, 2 * ROWS, 2 * LANES), jnp.bfloat16),
+            pltpu.VMEM((FIRST, ROWS, LANES), jnp.bfloat16),
+        ],
+        compiler_params=PARAMS,
+        cost_estimate=COST,
+        name="conv_part",
+    )(signal_blocks, taps_blocks, forward, inverse)
+
+
+def grad_call(gated_blocks, spec, filt, forward, inverse):
+    block = (CTX, ROWS, LANES)
+    return pl.pallas_call(
+        grad_kernel,
+        grid=(FIRST,),
+        in_specs=[
+            whole_spec(block),
+            each_spec((ROWS, LANES)),
+            each_spec((ROWS, LANES)),
+            TABLE_SPEC,
+            TABLE_SPEC,
+        ],
+        out_specs=[whole_spec(block), whole_spec((CTX, ROWS, HALF))],
+        out_shape=[
+            jax.ShapeDtypeStruct(block, jnp.bfloat16),
+            jax.ShapeDtypeStruct((CTX, ROWS, HALF), jnp.bfloat16),
+        ],
+        scratch_shapes=[
+            pltpu.VMEM((FIRST, 2 * ROWS, LANES), jnp.bfloat16),
+            pltpu.VMEM((FIRST, ROWS, 2 * LANES), jnp.bfloat16),
+        ],
+        compiler_params=PARAMS,
+        cost_estimate=COST,
+        name="grad_part",
+    )(gated_blocks, spec, filt, forward, inverse)
+
+
+def pack_pair(values, p):
+    offset = CTX * HALF
+    return jnp.concatenate(
+        [values[:, HALF * p : HALF * p + HALF], values[:, offset + HALF * p : offset + HALF * p + HALF]],
+        axis=1,
+    )
+
+
+def pack_kernel(signal_ref, packed_ref):
+    values = signal_ref[...].astype(jnp.float32)
+    for p in range(CTX):
+        packed_ref[p] = pack_pair(values, p).astype(jnp.bfloat16)
+
+
+def pack_gated_kernel(gate_ref, cotangent_ref, packed_ref):
+    values = cotangent_ref[...].astype(jnp.float32) * gate_ref[...].astype(jnp.float32)
+    for p in range(CTX):
+        packed_ref[p] = pack_pair(values, p).astype(jnp.bfloat16)
+
+
+PACK_ROWS = 128
+
+
+def row_spec(width):
+    return pl.BlockSpec((PACK_ROWS, width), lambda i: (i, 0))
+
+
+def packed_spec():
+    return pl.BlockSpec((CTX, PACK_ROWS, LANES), lambda i: (0, i, 0))
+
+
+def pack_call(body, arrays):
+    return pl.pallas_call(
+        body,
+        grid=(ROWS // PACK_ROWS,),
+        in_specs=[row_spec(array.shape[1]) for array in arrays],
+        out_specs=packed_spec(),
+        out_shape=jax.ShapeDtypeStruct((CTX, ROWS, LANES), jnp.bfloat16),
+        name="pack",
+    )(*arrays)
+
+
+def unpack(ref):
+    blocks = [ref[p].astype(jnp.float32) for p in range(CTX)]
+    return jnp.concatenate(
+        [block[:, :HALF] for block in blocks] + [block[:, HALF:] for block in blocks], axis=1
+    )
+
+
+def outputs_kernel(conv_ref, signal_ref, gate_ref, cotangent_ref, gain_ref, output_ref, gate_out_ref):
+    conv = unpack(conv_ref) + gain_ref[...] * signal_ref[...].astype(jnp.float32)
+    output_ref[...] = (gate_ref[...].astype(jnp.float32) * conv).astype(jnp.bfloat16)
+    gate_out_ref[...] = (cotangent_ref[...].astype(jnp.float32) * conv).astype(jnp.bfloat16)
+
+
+def signal_grad_kernel(grad_ref, gate_ref, cotangent_ref, gain_ref, out_ref):
+    gated = (cotangent_ref[...].astype(jnp.float32) * gate_ref[...].astype(jnp.float32)).astype(
+        jnp.bfloat16
+    )
+    out_ref[...] = (unpack(grad_ref) + gain_ref[...] * gated.astype(jnp.float32)).astype(jnp.bfloat16)
+
+
+def finish_call(body, packed, arrays, gain, count):
+    width = gain.shape[1]
+    return pl.pallas_call(
+        body,
+        grid=(ROWS // PACK_ROWS,),
+        in_specs=[packed_spec()]
+        + [row_spec(width)] * len(arrays)
+        + [pl.BlockSpec((1, width), lambda i: (0, 0))],
+        out_specs=[row_spec(width)] * count,
+        out_shape=[jax.ShapeDtypeStruct((ROWS, width), jnp.bfloat16)] * count,
+        name="finish",
+    )(packed, *arrays, gain)
+
+
+def exchange(blocks):
+    return lax.all_to_all(blocks, "ctx", split_axis=0, concat_axis=0, tiled=True)
+
+
+def per_device(signal, gate, filter_taps, skip_gain, out_cotangent):
+    filters = filter_taps.shape[1] * lax.axis_size("grp")
+    if (
+        lax.axis_size("ctx") != CTX
+        or signal.shape != (ROWS, 2 * filters)
+        or filters != CTX * HALF
+    ):
+        return per_device_general(signal, gate, filter_taps, skip_gain, out_cotangent)
+    forward, inverse = (jnp.asarray(table) for table in dense_tables())
+    gain = skip_gain[None, :]
+    all_taps = lax.all_gather(filter_taps, "grp", axis=1, tiled=True)
+    taps_blocks = exchange(all_taps.reshape(ROWS, CTX, HALF).transpose(1, 0, 2))
+    signal_blocks = exchange(pack_call(pack_kernel, [signal]))
+    gated_blocks = exchange(pack_call(pack_gated_kernel, [gate, out_cotangent]))
+    conv, spec, filt = conv_call(signal_blocks, taps_blocks, forward, inverse)
+    conv_back = exchange(conv)
+    grad, taps_grad = grad_call(gated_blocks, spec, filt, forward, inverse)
+    taps_back = exchange(taps_grad).transpose(1, 0, 2).reshape(ROWS, filters)
+    grad_back = exchange(grad)
+    output, grad_gate = finish_call(
+        outputs_kernel, conv_back, [signal, gate, out_cotangent], gain, 2
+    )
+    (grad_signal,) = finish_call(signal_grad_kernel, grad_back, [gate, out_cotangent], gain, 1)
+    scale = 1.0 / math.sqrt(CTX * ROWS * signal.shape[1] * lax.axis_size("grp") / filters)
+    grad_filter = lax.psum_scatter(taps_back, "grp", scatter_dimension=1, tiled=True)
+    return (output, grad_gate, grad_signal, grad_filter.astype(jnp.float32) * scale)
+
+
 def solution(mesh):
     placed = (P("ctx", "grp"), P("ctx", "grp"), P("ctx", "grp"), P("grp"), P("ctx", "grp"))
     return jax.shard_map(

time: 570 us -> 215 us (0.38)
  matrix products: 119 us -> 0 us
  local copies, waits for them, and re-layouts: 122 us -> 6.66 us
  Pallas kernels: 0 us -> 97.4 us
  other arithmetic: 98.1 us -> 0.93 us
  waiting for transfers between devices: 141 us -> 44.2 us
  starting transfers between devices: 51.9 us -> 18 us
  blocking collectives: 16.9 us -> 31.8 us
    dot_general x18 -> x0, matrix products: 119 us -> none  [the longest x3 29.2 us: inverse_front(): jnp.einsum('jb,pkjc->pkbc', sine_rows, operand, preferred_element_type=jn...]
    pallas_call x0 -> x6, Pallas kernels: none -> 97.4 us  [the longest x1 41.8 us: conv_call(): pl.pallas_call(conv_kernel, grid=(FIRST,), in_specs=[whole_spec(block), w...]
    all_to_all x12 -> x5, waiting for transfers between devices: 141 us -> 43.5 us  [exchange(): lax.all_to_all(blocks, 'ctx', split_axis=0, concat_axis=0, tiled=True)]
    all_to_all x12 -> x1, local copies, waits for them, and re-layouts: 48.6 us -> 1.32 us  [exchange(): lax.all_to_all(blocks, 'ctx', split_axis=0, concat_axis=0, tiled=True)]
    another operation x6 -> x0, local copies, waits for them, and re-layouts: 37.9 us -> none  [the longest x3 26.8 us: inverse_front(): jnp.stack([real_turned * twiddle_real + imag_turned * twiddle_imag, imag_...]
    all_to_all x12 -> x5, starting transfers between devices: 51.9 us -> 18 us  [exchange(): lax.all_to_all(blocks, 'ctx', split_axis=0, concat_axis=0, tiled=True)]
    another operation x17 -> x0, other arithmetic: 32.5 us -> none
    add x6 -> x0, other arithmetic: 30.4 us -> none  [the longest x2 21.2 us: second_forward(): with_cosine[1] + with_sine[0]]
  transfers between devices with their start and end apart: 13 -> 6, of which waited for: 8 -> 4; matrix products, arithmetic and copies ran while one was open for 38% -> 1% of each run, Pallas kernels for 0% -> 27%
where the time goes in v1:
time: 215 us; the launch traced here: 213 us
  Pallas kernels  97.4 us (45%)
  waiting for transfers between devices  44.2 us (21%)
  blocking collectives  31.8 us (15%)
  starting transfers between devices  18 us (8%)
  between operations  14.1 us (7%)
  local copies, waits for them, and re-layouts  6.66 us (3%)
    all_to_all x5, waiting for transfers between devices, exchange(): lax.all_to_all(blocks, 'ctx', split_axis=0, concat_axis=0, tiled=True)  43.5 us
    pallas_call x1, Pallas kernels, conv_call(): pl.pallas_call(conv_kernel, grid=(FIRST,), in_specs=[whole_spec(block), w...  41.8 us
    pallas_call x1, Pallas kernels, grad_call(): pl.pallas_call(grad_kernel, grid=(FIRST,), in_specs=[whole_spec(block), e...  39.5 us
    all_gather x1, blocking collectives, per_device(): all_taps = lax.all_gather(filter_taps, 'grp', axis=1, tiled=True)  18 us
    all_to_all x5, starting transfers between devices, exchange(): lax.all_to_all(blocks, 'ctx', split_axis=0, concat_axis=0, tiled=True)  18 us
    all_to_all x1, blocking collectives, exchange(): lax.all_to_all(blocks, 'ctx', split_axis=0, concat_axis=0, tiled=True)  13.8 us
    pallas_call x2, Pallas kernels, finish_call(): pl.pallas_call(body, grid=(ROWS // PACK_ROWS,), in_specs=[packed_spec()]...  8.67 us
    pallas_call x2, Pallas kernels, pack_call(): pl.pallas_call(body, grid=(ROWS // PACK_ROWS,), in_specs=[row_spec(array....  7.42 us
  transfers between devices with their start and end apart: 6, of which 4 were waited for; matrix products, arithmetic and copies ran while one was open for 1% of the time, Pallas kernels for 27%

profile of v1, /device:TPU:0, one launch (start us, length us, event | category | flops | bytes accessed | tf_op | source)
XLA Modules:
  0.0 213.0 jit_solution(13373945497630559774)
XLA Ops:
  7.2 1.0 copy.15
  8.2 18.0 %all_gather.3 = bf16[512,512]{0,1:T(8,128)(2,1)} all-gather(bf16[512,128]{0,1:T(8,128)(2,1)S(1)} %copy.15), channel_id=1, replica_groups=mesh['ctx'=8,'grp'=4] {'grp'}, dimensions={1}, use_global_device_ids=true | all-gather | bytes 655360 | tf_op jit(solution)/shard_map/all_gather | solution.py:626
  26.2 3.7 %all-to-all-start.1 = ((bf16[8,512,64]{1,2,0:T(8,128)(2,1)}), bf16[8,512,64]{1,2,0:T(8,128)(2,1)S(1)}, u32[]{:S(2)}, u32[]{:S(2)}) async-start(bf16[8,512,64]{1,2,0:T(8,128)(2,1)} %bitcast.1), calls=%async_computation.1 | async-start | bytes 1048576 | tf_op jit(solution)/shard_map/all_to_all | solution.py:613
  29.9 3.6 %pack.2 = bf16[8,512,128]{2,1,0:T(8,128)(2,1)} custom-call(bf16[512,1024]{1,0:T(8,128)(2,1)} %signal_ref.3), custom_call_target="tpu_custom_call" | custom-call | tf_op jit(solution)/shard_map/pack/pallas_call | solution.py:568
  33.5 6.1 %all-to-all-done.1 = bf16[8,512,64]{1,2,0:T(8,128)(2,1)S(1)} async-done(((bf16[8,512,64]{1,2,0:T(8,128)(2,1)}), bf16[8,512,64]{1,2,0:T(8,128)(2,1)S(1)}, u32[]{:S(2)}, u32[]{:S(2)}) %all-to-all-start.1) | async-done | bytes 524320 | tf_op jit(solution)/shard_map/all_to_all | solution.py:613
  39.6 3.6 %all-to-all-start = ((bf16[8,512,128]{2,1,0:T(8,128)(2,1)}), bf16[8,512,128]{2,1,0:T(8,128)(2,1)S(1)}, u32[]{:S(2)}, u32[]{:S(2)}) async-start(bf16[8,512,128]{2,1,0:T(8,128)(2,1)} %pack.2), calls=%async_computation | async-start | bytes 2097152 | tf_op jit(solution)/shard_map/all_to_all | solution.py:613
  43.2 3.8 %pack.3 = bf16[8,512,128]{2,1,0:T(8,128)(2,1)} custom-call(bf16[512,1024]{1,0:T(8,128)(2,1)} %gate_ref.5, bf16[512,1024]{1,0:T(8,128)(2,1)} %cotangent_ref.5), custom_call_target="tpu_custom_call" | custom-call | tf_op jit(solution)/shard_map/pack/pallas_call | solution.py:568
  47.0 11.5 %all-to-all-done.signal_ref = bf16[8,512,128]{2,1,0:T(8,128)(2,1)S(1)} async-done(((bf16[8,512,128]{2,1,0:T(8,128)(2,1)}), bf16[8,512,128]{2,1,0:T(8,128)(2,1)S(1)}, u32[]{:S(2)}, u32[]{:S(2)}) %all-to-all-start) | async-done | bytes 1048608 | tf_op jit(solution)/shard_map/all_to_all | solution.py:613
  58.5 0.0 copy-start.2
  58.6 3.6 %all-to-all-start.3 = ((bf16[8,512,128]{2,1,0:T(8,128)(2,1)}), bf16[8,512,128]{2,1,0:T(8,128)(2,1)S(1)}, u32[]{:S(2)}, u32[]{:S(2)}) async-start(bf16[8,512,128]{2,1,0:T(8,128)(2,1)} %pack.3), calls=%async_computation.3 | async-start | bytes 2097152 | tf_op jit(solution)/shard_map/all_to_all | solution.py:613
  62.1 1.3 copy.16.taps_ref
  63.4 0.0 copy-done.2
  63.4 41.8 %conv_part.1 = (bf16[8,512,128]{2,1,0:T(8,128)(2,1)}, bf16[16,512,128]{2,1,0:T(8,128)(2,1)}, bf16[16,512,128]{2,1,0:T(8,128)(2,1)}) custom-call(bf16[8,512,128]{2,1,0:T(8,128)(2,1)} %copy-done.2, bf16[8,512,64]{2,1,0:T(8,128)(2,1)} %copy.16.taps_ref, bf16[16,512,1024]{2,1,0:T(8,128)(2,1)} %constant.6.clone.forward_ref, ...), custom_call_target="tpu_custom_call" | custom-call | flops 8589934592 | bytes 41943040 | tf_op jit(solution)/shard_map/conv_part/pallas_call | solution.py:489
  105.2 0.0 all-to-all-done.3.gated_ref
  105.2 0.0 copy-start.1
  105.2 1.0 copy-done.1
  106.2 39.5 %grad_part.1 = (bf16[8,512,128]{2,1,0:T(8,128)(2,1)}, bf16[8,512,64]{2,1,0:T(8,128)(2,1)}) custom-call(bf16[8,512,128]{2,1,0:T(8,128)(2,1)} %copy-done.1, bf16[16,512,128]{2,1,0:T(8,128)(2,1)} %get-tuple-element.14.spec_ref, bf16[16,512,128]{2,1,0:T(8,128)(2,1)} %get-tuple-element.15.filt_ref, bf16[16,512,1024]{2,1,0:T(8,128)(2,1)} %constant.6.clone.forward_ref, ...), custom_call_target="tpu_custom_call" | custom-call | flops 8589934592 | bytes 41943040 | tf_op jit(solution)/shard_map/grad_part/pallas_call | solution.py:511
  145.7 1.5 copy.17
  147.2 13.8 %all_to_all.30 = bf16[8,512,64]{1,2,0:T(8,128)(2,1)} all-to-all(bf16[8,512,64]{1,2,0:T(8,128)(2,1)S(1)} %copy.17), channel_id=1, replica_groups=mesh['ctx'=8,'grp'=4] {'ctx'}, dimensions={0} | all-to-all | bytes 1048576 | tf_op jit(solution)/shard_map/all_to_all | solution.py:613
  161.0 3.6 %all-to-all-start.4 = ((bf16[8,512,128]{2,1,0:T(8,128)(2,1)}), bf16[8,512,128]{2,1,0:T(8,128)(2,1)S(1)}, u32[]{:S(2)}, u32[]{:S(2)}) async-start(bf16[8,512,128]{2,1,0:T(8,128)(2,1)} %get-tuple-element.16), calls=%async_computation.4 | async-start | bytes 2097152 | tf_op jit(solution)/shard_map/all_to_all | solution.py:613
  164.6 0.0 reduce-scatter.2.cloned.1.call-start
  164.6 0.7 reduce-scatter.2.cloned.1.call-update
  165.3 14.6 %all-to-all-done.4.grad_ref = bf16[8,512,128]{2,1,0:T(8,128)(2,1)S(1)} async-done(((bf16[8,512,128]{2,1,0:T(8,128)(2,1)}), bf16[8,512,128]{2,1,0:T(8,128)(2,1)S(1)}, u32[]{:S(2)}, u32[]{:S(2)}) %all-to-all-start.4) | async-done | bytes 1048608 | tf_op jit(solution)/shard_map/all_to_all | solution.py:613
  179.9 0.0 copy-start
  179.9 3.6 %all-to-all-start.2 = ((bf16[8,512,128]{2,1,0:T(8,128)(2,1)}), bf16[8,512,128]{2,1,0:T(8,128)(2,1)S(1)}, u32[]{:S(2)}, u32[]{:S(2)}) async-start(bf16[8,512,128]{2,1,0:T(8,128)(2,1)} %get-tuple-element.11), calls=%async_computation.2 | async-start | bytes 2097152 | tf_op jit(solution)/shard_map/all_to_all | solution.py:613
  183.5 0.0 copy-done
  183.5 4.1 %finish.3 = bf16[512,1024]{1,0:T(8,128)(2,1)} custom-call(bf16[8,512,128]{2,1,0:T(8,128)(2,1)} %copy-done, bf16[512,1024]{1,0:T(8,128)(2,1)} %gate_ref.5, bf16[512,1024]{1,0:T(8,128)(2,1)} %cotangent_ref.5, f32[1,1024]{1,0:T(1,128)} %bitcast.8), custom_call_target="tpu_custom_call" | custom-call | tf_op jit(solution)/shard_map/finish/pallas_call | solution.py:600
  187.6 11.2 %all-to-all-done.2.conv_ref = bf16[8,512,128]{2,1,0:T(8,128)(2,1)S(1)} async-done(((bf16[8,512,128]{2,1,0:T(8,128)(2,1)}), bf16[8,512,128]{2,1,0:T(8,128)(2,1)S(1)}, u32[]{:S(2)}, u32[]{:S(2)}) %all-to-all-start.2) | async-done | bytes 1048608 | tf_op jit(solution)/shard_map/all_to_all | solution.py:613
  198.8 1.0 copy-done.3
  199.8 4.6 %finish.2 = (bf16[512,1024]{1,0:T(8,128)(2,1)}, bf16[512,1024]{1,0:T(8,128)(2,1)}) custom-call(bf16[8,512,128]{2,1,0:T(8,128)(2,1)} %copy-done.3, bf16[512,1024]{1,0:T(8,128)(2,1)} %signal_ref.3, bf16[512,1024]{1,0:T(8,128)(2,1)} %gate_ref.5, bf16[512,1024]{1,0:T(8,128)(2,1)} %cotangent_ref.5, f32[1,1024]{1,0:T(1,128)} %bitcast.9), custom_call_target="tpu_custom_call" | custom-call | tf_op jit(solution)/shard_map/finish/pallas_call | solution.py:600
  204.4 0.9 convert_multiply_fusion
  205.3 0.8 copy.18
  (2 shorter events, 0.0 us)
Async XLA Ops:
  26.2 13.5 %all-to-all-start.1 = ((bf16[8,512,64]{1,2,0:T(8,128)(2,1)}), bf16[8,512,64]{1,2,0:T(8,128)(2,1)S(1)}, u32[]{:S(2)}, u32[]{:S(2)}) async-start(bf16[8,512,64]{1,2,0:T(8,128)(2,1)} %bitcast.1), calls=%async_computation.1 | async-start | bytes 1048576 | tf_op jit(solution)/shard_map/all_to_all | solution.py:613
  39.6 18.9 %all-to-all-start = ((bf16[8,512,128]{2,1,0:T(8,128)(2,1)}), bf16[8,512,128]{2,1,0:T(8,128)(2,1)S(1)}, u32[]{:S(2)}, u32[]{:S(2)}) async-start(bf16[8,512,128]{2,1,0:T(8,128)(2,1)} %pack.2), calls=%async_computation | async-start | bytes 2097152 | tf_op jit(solution)/shard_map/all_to_all | solution.py:613
  58.5 4.9 %copy-start.2 = (bf16[8,512,128]{2,1,0:T(8,128)(2,1)}, bf16[8,512,128]{2,1,0:T(8,128)(2,1)S(1)}, u32[]{:S(2)}) copy-start(bf16[8,512,128]{2,1,0:T(8,128)(2,1)S(1)} %all-to-all-done.signal_ref) | copy-start | bytes 3145732
  58.6 46.7 %all-to-all-start.3 = ((bf16[8,512,128]{2,1,0:T(8,128)(2,1)}), bf16[8,512,128]{2,1,0:T(8,128)(2,1)S(1)}, u32[]{:S(2)}, u32[]{:S(2)}) async-start(bf16[8,512,128]{2,1,0:T(8,128)(2,1)} %pack.3), calls=%async_computation.3 | async-start | bytes 2097152 | tf_op jit(solution)/shard_map/all_to_all | solution.py:613
  105.2 1.0 copy-start.1
  161.0 18.9 %all-to-all-start.4 = ((bf16[8,512,128]{2,1,0:T(8,128)(2,1)}), bf16[8,512,128]{2,1,0:T(8,128)(2,1)S(1)}, u32[]{:S(2)}, u32[]{:S(2)}) async-start(bf16[8,512,128]{2,1,0:T(8,128)(2,1)} %get-tuple-element.16), calls=%async_computation.4 | async-start | bytes 2097152 | tf_op jit(solution)/shard_map/all_to_all | solution.py:613
  164.6 39.8 %reduce-scatter.2.cloned.1.call-start = ((), (), s32[]{:S(2)}) async-start(), calls=%async_computation.7 | async-start | bytes 655360 | tf_op jit(solution)/shard_map/reduce_scatter | solution.py:640
  179.9 3.6 %copy-start = (bf16[8,512,128]{2,1,0:T(8,128)(2,1)}, bf16[8,512,128]{2,1,0:T(8,128)(2,1)S(1)}, u32[]{:S(2)}) copy-start(bf16[8,512,128]{2,1,0:T(8,128)(2,1)S(1)} %all-to-all-done.4.grad_ref) | copy-start | bytes 3145732
  179.9 18.9 %all-to-all-start.2 = ((bf16[8,512,128]{2,1,0:T(8,128)(2,1)}), bf16[8,512,128]{2,1,0:T(8,128)(2,1)S(1)}, u32[]{:S(2)}, u32[]{:S(2)}) async-start(bf16[8,512,128]{2,1,0:T(8,128)(2,1)} %get-tuple-element.11), calls=%async_computation.2 | async-start | bytes 2097152 | tf_op jit(solution)/shard_map/all_to_all | solution.py:613
  198.8 1.0 copy-start.3
Sparse Core Ops, SparseCore 0:
  167.7 23.8 reduce-scatter.1

commit v2 on v1

--- a/solution.py
+++ b/solution.py
@@ -242,6 +242,7 @@
 LANES = 128
 HALF = 64
 STRIP = 16
+PER_STEP = 4
 
 
 def low(values):
@@ -260,15 +261,10 @@
 def dense_tables():
     index = np.arange(ROWS)
     angles = (index[:, None] * index[None, :] % ROWS).astype(np.float32) * np.float32(TWO_PI / ROWS)
-    wide = low(np.cos(angles)).astype(np.float64) - 1j * low(np.sin(angles)).astype(np.float64)
-    freq = np.arange(FIRST)
-    padded = FIRST * ROWS
-    turn = np.exp(-2j * np.pi * (freq[:, None] * index[None, :] % padded) / padded)
-    both = wide[None] * turn[:, None, :]
-    forward = low(np.concatenate([both.real, both.imag], axis=2))
-    back = both.transpose(0, 2, 1) / padded
-    inverse = low(np.concatenate([back.real, -back.imag], axis=2))
-    return forward, inverse
+    table = low(np.concatenate([np.cos(angles), -np.sin(angles)], axis=1))
+    turn = index * (TWO_PI / (FIRST * ROWS))
+    turns = np.stack([np.cos(turn), -np.sin(turn)])[:, :, None]
+    return table, np.broadcast_to(turns, (2, ROWS, LANES)).astype(np.float32)
 
 
 COS, SIN = first_coefficients()
@@ -316,12 +312,13 @@
         else:
             real = scaled_sum([(1.0, blocks[0])] + [(COS[k, a], minus[a]) for a in (1, 2, 3)])
             turned = scaled_sum([(-SIN[k, 4], blocks[4])] + [(-SIN[k, a], plus[a]) for a in (1, 2, 3)])
+        real_turned = times_i(real, sign)
         if turned is None:
-            results[k] = real
+            results[k] = (real, real_turned)
             continue
-        turned = times_i(turned, sign)
-        results[k] = real + turned
-        results[FIRST - k] = real - turned
+        twice = times_i(turned, sign)
+        results[k] = (real + twice, real_turned - turned)
+        results[FIRST - k] = (real - twice, real_turned + turned)
     return results
 
 
@@ -353,112 +350,133 @@
     return jnp.where(lower_half((1, LANES)), -1.0, 1.0).astype(jnp.float32)
 
 
-def store_stacked(ref, k, rows, lanes, values, sign):
-    top = pl.ds(rows, values.shape[0])
-    bottom = pl.ds(ROWS + rows, values.shape[0])
-    ref[k, top, lanes] = values.astype(jnp.bfloat16)
-    ref[k, bottom, lanes] = times_i(values, sign).astype(jnp.bfloat16)
-
-
-def stage_one(load, stacked_ref, lane_start):
+def next_turn(turn, unit):
+    return (turn[0] * unit[0] - turn[1] * unit[1], turn[0] * unit[1] + turn[1] * unit[0])
+
+
+def stage_one(load, turns_ref, stacked_ref, lane_start):
     sign = signs()
 
     @pl.loop(0, ROWS // STRIP)
     def _(strip):
         rows = pl.multiple_of(strip * STRIP, STRIP)
         blocks = [load(a, pl.ds(rows, STRIP)) for a in range(CTX)]
-        for k, values in enumerate(forward_first(blocks, sign)):
-            store_stacked(
-                stacked_ref, k, rows, slice(lane_start, lane_start + LANES), values, sign
-            )
-
-
-def last_stage(half_ref, lane_start, store):
+        unit = (turns_ref[0, pl.ds(rows, STRIP), :], turns_ref[1, pl.ds(rows, STRIP), :])
+        lanes = slice(lane_start, lane_start + LANES)
+        turn = None
+        for k, (values, turned) in enumerate(forward_first(blocks, sign)):
+            if k > 0:
+                turn = unit if turn is None else next_turn(turn, unit)
+                values, turned = (
+                    values * turn[0] + turned * turn[1],
+                    turned * turn[0] - values * turn[1],
+                )
+            stacked_ref[k, pl.ds(rows, STRIP), lanes] = values.astype(jnp.bfloat16)
+            stacked_ref[k, pl.ds(ROWS + rows, STRIP), lanes] = turned.astype(jnp.bfloat16)
+
+
+def last_stage(half_ref, turns_ref, lane_start, store):
     sign = signs()
 
     @pl.loop(0, ROWS // STRIP)
     def _(strip):
         rows = pl.multiple_of(strip * STRIP, STRIP)
-        parts = [
-            half_ref[k, pl.ds(rows, STRIP), lane_start : lane_start + LANES].astype(jnp.float32)
-            for k in range(FIRST)
-        ]
+        unit = (turns_ref[0, pl.ds(rows, STRIP), :], turns_ref[1, pl.ds(rows, STRIP), :])
+        turn = (1.0 / (FIRST * ROWS), 0.0)
+        parts = []
+        for k in range(FIRST):
+            part = half_ref[k, pl.ds(rows, STRIP), lane_start : lane_start + LANES].astype(
+                jnp.float32
+            )
+            if k == 0:
+                parts.append(part * turn[0])
+                continue
+            turn = (turn[0] * unit[0], turn[0] * unit[1]) if k == 1 else next_turn(turn, unit)
+            parts.append(part * turn[0] - times_i(part, sign) * turn[1])
         for a, values in enumerate(inverse_last(parts, sign)):
             store(a, pl.ds(rows, STRIP), values)
 
 
-def conv_kernel(signal_ref, taps_ref, forward_ref, inverse_ref, conv_ref, spec_ref, filt_ref,
+def conv_kernel(signal_ref, taps_ref, table_ref, turns_ref, conv_ref, spec_ref, filt_ref,
                 stacked, half):
     k = pl.program_id(0)
 
     @pl.when(k == 0)
     def _():
-        stage_one(lambda a, rows: signal_ref[a, rows, :].astype(jnp.float32), stacked, 0)
+        stage_one(lambda a, rows: signal_ref[a, rows, :].astype(jnp.float32), turns_ref, stacked, 0)
 
         def load_taps(a, rows):
             values = taps_ref[a, rows, :].astype(jnp.float32)
             return jnp.concatenate([values, jnp.zeros_like(values)], axis=1)
 
-        stage_one(load_taps, stacked, LANES)
+        stage_one(load_taps, turns_ref, stacked, LANES)
 
     sign = signs()
-    spectra = jnp.dot(forward_ref[0], stacked[k], preferred_element_type=jnp.float32)
-    signal_spec = spectra[:, :LANES]
-    filter_low = spectra[:, LANES:].astype(jnp.bfloat16)
-    spec_ref[0] = signal_spec.astype(jnp.bfloat16)
-    filt_ref[0] = filter_low
-    filter_wide = filter_low.astype(jnp.float32)
-    swapped = swap(filter_wide)
-    first_half = lower_half((ROWS, LANES))
-    filter_real = jnp.where(first_half, filter_wide, swapped)
-    filter_imag = jnp.where(first_half, swapped, filter_wide)
-    product = signal_spec * filter_real + times_i(signal_spec, sign) * filter_imag
-    operand = jnp.concatenate([product, times_i(product, sign)], axis=0).astype(jnp.bfloat16)
-    half[k] = jnp.dot(inverse_ref[0], operand, preferred_element_type=jnp.float32).astype(
-        jnp.bfloat16
-    )
-
-    @pl.when(k == FIRST - 1)
+    all_spectra = [
+        jnp.dot(table_ref[...], stacked[k * PER_STEP + sub], preferred_element_type=jnp.float32)
+        for sub in range(PER_STEP)
+    ]
+    for sub, spectra in enumerate(all_spectra):
+        signal_spec = spectra[:, :LANES]
+        filter_low = spectra[:, LANES:].astype(jnp.bfloat16)
+        spec_ref[sub] = signal_spec.astype(jnp.bfloat16)
+        filt_ref[sub] = filter_low
+        filter_wide = filter_low.astype(jnp.float32)
+        swapped = swap(filter_wide)
+        first_half = lower_half((ROWS, LANES))
+        filter_real = jnp.where(first_half, filter_wide, swapped)
+        filter_imag = jnp.where(first_half, swapped, filter_wide)
+        product = signal_spec * filter_real + times_i(signal_spec, sign) * filter_imag
+        operand = jnp.concatenate([product, times_i(product, -sign)], axis=0).astype(jnp.bfloat16)
+        half[k * PER_STEP + sub] = jnp.dot(table_ref[...], operand, preferred_element_type=jnp.float32).astype(
+            jnp.bfloat16
+        )
+
+    @pl.when(k == FIRST // PER_STEP - 1)
     def _():
         def store(a, rows, values):
             conv_ref[a, rows, :] = values.astype(jnp.bfloat16)
 
-        last_stage(half, 0, store)
-
-
-def grad_kernel(gated_ref, spec_ref, filt_ref, forward_ref, inverse_ref, grad_ref, taps_ref,
+        last_stage(half, turns_ref, 0, store)
+
+
+def grad_kernel(gated_ref, spec_ref, filt_ref, table_ref, turns_ref, grad_ref, taps_ref,
                 stacked, half):
     k = pl.program_id(0)
 
     @pl.when(k == 0)
     def _():
-        stage_one(lambda a, rows: gated_ref[a, rows, :].astype(jnp.float32), stacked, 0)
+        stage_one(lambda a, rows: gated_ref[a, rows, :].astype(jnp.float32), turns_ref, stacked, 0)
 
     sign = signs()
-    spectra = jnp.dot(forward_ref[0], stacked[k], preferred_element_type=jnp.float32)
-    turned = times_i(spectra, sign)
-    first_half = lower_half((ROWS, LANES))
-
-    def split(values):
-        swapped = swap(values)
-        return jnp.where(first_half, values, swapped), jnp.where(first_half, swapped, values)
-
-    filter_real, filter_imag = split(filt_ref[0].astype(jnp.float32))
-    signal_real, signal_imag = split(spec_ref[0].astype(jnp.float32))
-    back = spectra * filter_real - turned * filter_imag
-    cross = spectra * signal_real - turned * signal_imag
-    operand = jnp.concatenate(
-        [
-            jnp.concatenate([back, cross], axis=1),
-            jnp.concatenate([times_i(back, sign), times_i(cross, sign)], axis=1),
-        ],
-        axis=0,
-    ).astype(jnp.bfloat16)
-    half[k] = jnp.dot(inverse_ref[0], operand, preferred_element_type=jnp.float32).astype(
-        jnp.bfloat16
-    )
-
-    @pl.when(k == FIRST - 1)
+    all_spectra = [
+        jnp.dot(table_ref[...], stacked[k * PER_STEP + sub], preferred_element_type=jnp.float32)
+        for sub in range(PER_STEP)
+    ]
+    for sub, spectra in enumerate(all_spectra):
+        turned = times_i(spectra, sign)
+        first_half = lower_half((ROWS, LANES))
+
+        def split(values):
+            swapped = swap(values)
+            return jnp.where(first_half, values, swapped), jnp.where(first_half, swapped, values)
+
+        filter_real, filter_imag = split(filt_ref[sub].astype(jnp.float32))
+        signal_real, signal_imag = split(spec_ref[sub].astype(jnp.float32))
+        back = spectra * filter_real - turned * filter_imag
+        cross = spectra * signal_real - turned * signal_imag
+        operand = jnp.concatenate(
+            [
+                jnp.concatenate([back, cross], axis=1),
+                jnp.concatenate([times_i(back, -sign), times_i(cross, -sign)], axis=1),
+            ],
+            axis=0,
+        ).astype(jnp.bfloat16)
+        half[k * PER_STEP + sub] = jnp.dot(table_ref[...], operand, preferred_element_type=jnp.float32).astype(
+            jnp.bfloat16
+        )
+
+    @pl.when(k == FIRST // PER_STEP - 1)
     def _():
         def store(a, rows, values):
             grad_ref[a, rows, :] = values.astype(jnp.bfloat16)
@@ -466,8 +484,8 @@
         def store_taps(a, rows, values):
             taps_ref[a, rows, :] = values[:, :HALF].astype(jnp.bfloat16)
 
-        last_stage(half, 0, store)
-        last_stage(half, LANES, store_taps)
+        last_stage(half, turns_ref, 0, store)
+        last_stage(half, turns_ref, LANES, store_taps)
 
 
 def whole_spec(shape):
@@ -475,21 +493,21 @@
 
 
 def each_spec(shape):
-    return pl.BlockSpec((1,) + shape, lambda k: (k,) + (0,) * len(shape))
-
-
-TABLE_SPEC = each_spec((ROWS, 2 * ROWS))
+    return pl.BlockSpec((PER_STEP,) + shape, lambda k: (k,) + (0,) * len(shape))
+
+
+TABLE_SPECS = [whole_spec((ROWS, 2 * ROWS)), whole_spec((2, ROWS, LANES))]
 PARAMS = pltpu.CompilerParams(vmem_limit_bytes=56 * 1024 * 1024)
 WORK = 2 * FIRST * ROWS * 2 * ROWS * 2 * LANES * 2
-COST = pl.CostEstimate(flops=WORK, bytes_accessed=40 * 1024 * 1024, transcendentals=0)
-
-
-def conv_call(signal_blocks, taps_blocks, forward, inverse):
+COST = pl.CostEstimate(flops=WORK, bytes_accessed=60 * 1024 * 1024, transcendentals=0)
+
+
+def conv_call(signal_blocks, taps_blocks, table, turns):
     block = (CTX, ROWS, LANES)
     return pl.pallas_call(
         conv_kernel,
-        grid=(FIRST,),
-        in_specs=[whole_spec(block), whole_spec((CTX, ROWS, HALF)), TABLE_SPEC, TABLE_SPEC],
+        grid=(FIRST // PER_STEP,),
+        in_specs=[whole_spec(block), whole_spec((CTX, ROWS, HALF))] + TABLE_SPECS,
         out_specs=[whole_spec(block), each_spec((ROWS, LANES)), each_spec((ROWS, LANES))],
         out_shape=[
             jax.ShapeDtypeStruct(block, jnp.bfloat16),
@@ -503,21 +521,20 @@
         compiler_params=PARAMS,
         cost_estimate=COST,
         name="conv_part",
-    )(signal_blocks, taps_blocks, forward, inverse)
-
-
-def grad_call(gated_blocks, spec, filt, forward, inverse):
+    )(signal_blocks, taps_blocks, table, turns)
+
+
+def grad_call(gated_blocks, spec, filt, table, turns):
     block = (CTX, ROWS, LANES)
     return pl.pallas_call(
         grad_kernel,
-        grid=(FIRST,),
+        grid=(FIRST // PER_STEP,),
         in_specs=[
             whole_spec(block),
             each_spec((ROWS, LANES)),
             each_spec((ROWS, LANES)),
-            TABLE_SPEC,
-            TABLE_SPEC,
-        ],
+        ]
+        + TABLE_SPECS,
         out_specs=[whole_spec(block), whole_spec((CTX, ROWS, HALF))],
         out_shape=[
             jax.ShapeDtypeStruct(block, jnp.bfloat16),
@@ -530,7 +547,7 @@
         compiler_params=PARAMS,
         cost_estimate=COST,
         name="grad_part",
-    )(gated_blocks, spec, filt, forward, inverse)
+    )(gated_blocks, spec, filt, table, turns)
 
 
 def pack_pair(values, p):
@@ -621,15 +638,16 @@
         or filters != CTX * HALF
     ):
         return per_device_general(signal, gate, filter_taps, skip_gain, out_cotangent)
-    forward, inverse = (jnp.asarray(table) for table in dense_tables())
+    table, turns = (jnp.asarray(table) for table in dense_tables())
     gain = skip_gain[None, :]
     all_taps = lax.all_gather(filter_taps, "grp", axis=1, tiled=True)
     taps_blocks = exchange(all_taps.reshape(ROWS, CTX, HALF).transpose(1, 0, 2))
     signal_blocks = exchange(pack_call(pack_kernel, [signal]))
     gated_blocks = exchange(pack_call(pack_gated_kernel, [gate, out_cotangent]))
-    conv, spec, filt = conv_call(signal_blocks, taps_blocks, forward, inverse)
+    conv, spec, filt = conv_call(signal_blocks, taps_blocks, table, turns)
     conv_back = exchange(conv)
-    grad, taps_grad = grad_call(gated_blocks, spec, filt, forward, inverse)
+    grad, taps_grad = grad_call(gated_blocks, spec, filt, table, turns)
+    grad, taps_grad, conv_back = lax.optimization_barrier((grad, taps_grad, conv_back))
     taps_back = exchange(taps_grad).transpose(1, 0, 2).reshape(ROWS, filters)
     grad_back = exchange(grad)
     output, grad_gate = finish_call(

time: 215 us -> 173 us (0.80)
  Pallas kernels: 97.4 us -> 72.4 us
  waiting for transfers between devices: 44.2 us -> 28.4 us
    pallas_call x2, Pallas kernels: 81.3 us -> 56.3 us  [the longest x1 29.2 us: grad_call(): pl.pallas_call(grad_kernel, grid=(FIRST // PER_STEP,), in_specs=[whole_sp...]
    all_to_all x5, waiting for transfers between devices: 43.5 us -> 28.4 us  [exchange(): lax.all_to_all(blocks, 'ctx', split_axis=0, concat_axis=0, tiled=True)]
  transfers between devices with their start and end apart: 6 -> 6, of which waited for: 4 -> 3; matrix products, arithmetic and copies ran while one was open for 1% -> 1% of each run, Pallas kernels for 27% -> 42%
where the time goes in v2:
time: 173 us; the launch traced here: 172 us
  Pallas kernels  72.4 us (42%)
  blocking collectives  31.8 us (18%)
  waiting for transfers between devices  28.4 us (16%)
  starting transfers between devices  18.6 us (11%)
  between operations  14.1 us (8%)
  local copies, waits for them, and re-layouts  6.08 us (4%)
    pallas_call x1, Pallas kernels, grad_call(): pl.pallas_call(grad_kernel, grid=(FIRST // PER_STEP,), in_specs=[whole_sp...  29.2 us
    all_to_all x5, waiting for transfers between devices, exchange(): lax.all_to_all(blocks, 'ctx', split_axis=0, concat_axis=0, tiled=True)  28.4 us
    pallas_call x1, Pallas kernels, conv_call(): pl.pallas_call(conv_kernel, grid=(FIRST // PER_STEP,), in_specs=[whole_sp...  27.1 us
    all_to_all x5, starting transfers between devices, exchange(): lax.all_to_all(blocks, 'ctx', split_axis=0, concat_axis=0, tiled=True)  18.5 us
    all_gather x1, blocking collectives, per_device(): all_taps = lax.all_gather(filter_taps, 'grp', axis=1, tiled=True)  18 us
    all_to_all x1, blocking collectives, exchange(): lax.all_to_all(blocks, 'ctx', split_axis=0, concat_axis=0, tiled=True)  13.8 us
    pallas_call x2, Pallas kernels, finish_call(): pl.pallas_call(body, grid=(ROWS // PACK_ROWS,), in_specs=[packed_spec()]...  8.68 us
    pallas_call x2, Pallas kernels, pack_call(): pl.pallas_call(body, grid=(ROWS // PACK_ROWS,), in_specs=[row_spec(array....  7.42 us
  transfers between devices with their start and end apart: 6, of which 3 were waited for; matrix products, arithmetic and copies ran while one was open for 1% of the time, Pallas kernels for 42%

profile of v2, /device:TPU:0, one launch (start us, length us, event | category | flops | bytes accessed | tf_op | source)
XLA Modules:
  0.0 172.4 jit_solution(6088413723821713599)
XLA Ops:
  7.2 1.0 copy.15
  8.2 18.0 %all_gather.3 = bf16[512,512]{0,1:T(8,128)(2,1)} all-gather(bf16[512,128]{0,1:T(8,128)(2,1)S(1)} %copy.15), channel_id=1, replica_groups=mesh['ctx'=8,'grp'=4] {'grp'}, dimensions={1}, use_global_device_ids=true | all-gather | bytes 655360 | tf_op jit(solution)/shard_map/all_gather | solution.py:643
  26.2 3.7 %all-to-all-start.2 = ((bf16[8,512,64]{1,2,0:T(8,128)(2,1)}), bf16[8,512,64]{1,2,0:T(8,128)(2,1)S(1)}, u32[]{:S(2)}, u32[]{:S(2)}) async-start(bf16[8,512,64]{1,2,0:T(8,128)(2,1)} %bitcast.1), calls=%async_computation.2 | async-start | bytes 1048576 | tf_op jit(solution)/shard_map/all_to_all | solution.py:630
  29.9 3.6 %pack.3 = bf16[8,512,128]{2,1,0:T(8,128)(2,1)} custom-call(bf16[512,1024]{1,0:T(8,128)(2,1)} %signal_ref.3), custom_call_target="tpu_custom_call" | custom-call | tf_op jit(solution)/shard_map/pack/pallas_call | solution.py:585
  33.5 6.1 %all-to-all-done.2 = bf16[8,512,64]{1,2,0:T(8,128)(2,1)S(1)} async-done(((bf16[8,512,64]{1,2,0:T(8,128)(2,1)}), bf16[8,512,64]{1,2,0:T(8,128)(2,1)S(1)}, u32[]{:S(2)}, u32[]{:S(2)}) %all-to-all-start.2) | async-done | bytes 524320 | tf_op jit(solution)/shard_map/all_to_all | solution.py:630
  39.6 3.6 %all-to-all-start.1 = ((bf16[8,512,128]{2,1,0:T(8,128)(2,1)}), bf16[8,512,128]{2,1,0:T(8,128)(2,1)S(1)}, u32[]{:S(2)}, u32[]{:S(2)}) async-start(bf16[8,512,128]{2,1,0:T(8,128)(2,1)} %pack.3), calls=%async_computation.1 | async-start | bytes 2097152 | tf_op jit(solution)/shard_map/all_to_all | solution.py:630
  43.2 3.8 %pack.2 = bf16[8,512,128]{2,1,0:T(8,128)(2,1)} custom-call(bf16[512,1024]{1,0:T(8,128)(2,1)} %gate_ref.5, bf16[512,1024]{1,0:T(8,128)(2,1)} %cotangent_ref.5), custom_call_target="tpu_custom_call" | custom-call | tf_op jit(solution)/shard_map/pack/pallas_call | solution.py:585
  47.0 11.5 %all-to-all-done.1.signal_ref = bf16[8,512,128]{2,1,0:T(8,128)(2,1)S(1)} async-done(((bf16[8,512,128]{2,1,0:T(8,128)(2,1)}), bf16[8,512,128]{2,1,0:T(8,128)(2,1)S(1)}, u32[]{:S(2)}, u32[]{:S(2)}) %all-to-all-start.1) | async-done | bytes 1048608 | tf_op jit(solution)/shard_map/all_to_all | solution.py:630
  58.5 0.0 copy-start.3
  58.6 3.6 %all-to-all-start = ((bf16[8,512,128]{2,1,0:T(8,128)(2,1)}), bf16[8,512,128]{2,1,0:T(8,128)(2,1)S(1)}, u32[]{:S(2)}, u32[]{:S(2)}) async-start(bf16[8,512,128]{2,1,0:T(8,128)(2,1)} %pack.2), calls=%async_computation | async-start | bytes 2097152 | tf_op jit(solution)/shard_map/all_to_all | solution.py:630
  62.1 1.3 copy.16.taps_ref
  63.4 0.0 copy-done.3
  63.4 27.1 %conv_part.1 = (bf16[8,512,128]{2,1,0:T(8,128)(2,1)}, bf16[16,512,128]{2,1,0:T(8,128)(2,1)}, bf16[16,512,128]{2,1,0:T(8,128)(2,1)}) custom-call(bf16[8,512,128]{2,1,0:T(8,128)(2,1)} %copy-done.3, bf16[8,512,64]{2,1,0:T(8,128)(2,1)} %copy.16.taps_ref, bf16[512,1024]{1,0:T(8,128)(2,1)} %constant.6.clone.table_ref, f32[2,512,128]{2,1,0:T(8,128)} %constant.7.clone.turns_ref), custom_call_target="tpu_custom_call" | custom-call | flops 8589934592 | bytes 62914560 | tf_op jit(solution)/shard_map/conv_part/pallas_call | solution.py:507
  90.6 0.0 all-to-all-done.gated_ref
  90.6 0.0 copy-start.2
  90.6 4.1 %all-to-all-start.3 = ((bf16[8,512,128]{2,1,0:T(8,128)(2,1)}), bf16[8,512,128]{2,1,0:T(8,128)(2,1)S(1)}, u32[]{:S(2)}, u32[]{:S(2)}) async-start(bf16[8,512,128]{2,1,0:T(8,128)(2,1)} %get-tuple-element.18), calls=%async_computation.3 | async-start | bytes 2097152 | tf_op jit(solution)/shard_map/all_to_all | solution.py:630
  94.7 0.0 reduce-scatter.2.cloned.1.call-start
  94.7 0.0 copy-done.2
  94.8 29.2 %grad_part.1 = (bf16[8,512,128]{2,1,0:T(8,128)(2,1)}, bf16[8,512,64]{2,1,0:T(8,128)(2,1)}) custom-call(bf16[8,512,128]{2,1,0:T(8,128)(2,1)} %copy-done.2, bf16[16,512,128]{2,1,0:T(8,128)(2,1)} %get-tuple-element.14.spec_ref, bf16[16,512,128]{2,1,0:T(8,128)(2,1)} %get-tuple-element.15.filt_ref, bf16[512,1024]{1,0:T(8,128)(2,1)} %constant.6.clone.table_ref, ...), custom_call_target="tpu_custom_call" | custom-call | flops 8589934592 | bytes 62914560 | tf_op jit(solution)/shard_map/grad_part/pallas_call | solution.py:529
  124.0 0.0 all-to-all-done.3.conv_ref
  124.0 0.0 copy-start
  124.0 1.9 %copy.17 = bf16[8,512,64]{1,2,0:T(8,128)(2,1)S(1)} copy(bf16[8,512,64]{2,1,0:T(8,128)(2,1)} %get-tuple-element.23) | data formatting | bytes 1048576 | tf_op jit(solution)/shard_map/optimization_barrier | solution.py:650
  125.9 13.8 %all_to_all.30 = bf16[8,512,64]{1,2,0:T(8,128)(2,1)} all-to-all(bf16[8,512,64]{1,2,0:T(8,128)(2,1)S(1)} %copy.17), channel_id=1, replica_groups=mesh['ctx'=8,'grp'=4] {'ctx'}, dimensions={0} | all-to-all | bytes 1048576 | tf_op jit(solution)/shard_map/all_to_all | solution.py:630
  139.7 0.0 reduce-scatter.2.cloned.1.call-update
  139.7 0.0 copy-done
  139.8 3.6 %all-to-all-start.4 = ((bf16[8,512,128]{2,1,0:T(8,128)(2,1)}), bf16[8,512,128]{2,1,0:T(8,128)(2,1)S(1)}, u32[]{:S(2)}, u32[]{:S(2)}) async-start(bf16[8,512,128]{2,1,0:T(8,128)(2,1)} %get-tuple-element.22), calls=%async_computation.4 | async-start | bytes 2097152 | tf_op jit(solution)/shard_map/all_to_all | solution.py:630
  143.3 4.6 %finish.2 = (bf16[512,1024]{1,0:T(8,128)(2,1)}, bf16[512,1024]{1,0:T(8,128)(2,1)}) custom-call(bf16[8,512,128]{2,1,0:T(8,128)(2,1)} %copy-done, bf16[512,1024]{1,0:T(8,128)(2,1)} %signal_ref.3, bf16[512,1024]{1,0:T(8,128)(2,1)} %gate_ref.5, bf16[512,1024]{1,0:T(8,128)(2,1)} %cotangent_ref.5, f32[1,1024]{1,0:T(1,128)} %bitcast.8), custom_call_target="tpu_custom_call" | custom-call | tf_op jit(solution)/shard_map/finish/pallas_call | solution.py:617
  147.9 10.7 %all-to-all-done.4.grad_ref = bf16[8,512,128]{2,1,0:T(8,128)(2,1)S(1)} async-done(((bf16[8,512,128]{2,1,0:T(8,128)(2,1)}), bf16[8,512,128]{2,1,0:T(8,128)(2,1)S(1)}, u32[]{:S(2)}, u32[]{:S(2)}) %all-to-all-start.4) | async-done | bytes 1048608 | tf_op jit(solution)/shard_map/all_to_all | solution.py:630
  158.7 1.0 copy-done.1
  159.7 4.1 %finish.3 = bf16[512,1024]{1,0:T(8,128)(2,1)} custom-call(bf16[8,512,128]{2,1,0:T(8,128)(2,1)} %copy-done.1, bf16[512,1024]{1,0:T(8,128)(2,1)} %gate_ref.5, bf16[512,1024]{1,0:T(8,128)(2,1)} %cotangent_ref.5, f32[1,1024]{1,0:T(1,128)} %bitcast.9), custom_call_target="tpu_custom_call" | custom-call | tf_op jit(solution)/shard_map/finish/pallas_call | solution.py:617
  163.8 0.9 convert_multiply_fusion
  164.7 0.8 copy.18
  (2 shorter events, 0.0 us)
Async XLA Ops:
  26.2 13.5 %all-to-all-start.2 = ((bf16[8,512,64]{1,2,0:T(8,128)(2,1)}), bf16[8,512,64]{1,2,0:T(8,128)(2,1)S(1)}, u32[]{:S(2)}, u32[]{:S(2)}) async-start(bf16[8,512,64]{1,2,0:T(8,128)(2,1)} %bitcast.1), calls=%async_computation.2 | async-start | bytes 1048576 | tf_op jit(solution)/shard_map/all_to_all | solution.py:630
  39.6 18.9 %all-to-all-start.1 = ((bf16[8,512,128]{2,1,0:T(8,128)(2,1)}), bf16[8,512,128]{2,1,0:T(8,128)(2,1)S(1)}, u32[]{:S(2)}, u32[]{:S(2)}) async-start(bf16[8,512,128]{2,1,0:T(8,128)(2,1)} %pack.3), calls=%async_computation.1 | async-start | bytes 2097152 | tf_op jit(solution)/shard_map/all_to_all | solution.py:630
  58.5 4.9 %copy-start.3 = (bf16[8,512,128]{2,1,0:T(8,128)(2,1)}, bf16[8,512,128]{2,1,0:T(8,128)(2,1)S(1)}, u32[]{:S(2)}) copy-start(bf16[8,512,128]{2,1,0:T(8,128)(2,1)S(1)} %all-to-all-done.1.signal_ref) | copy-start | bytes 3145732
  58.6 32.0 %all-to-all-start = ((bf16[8,512,128]{2,1,0:T(8,128)(2,1)}), bf16[8,512,128]{2,1,0:T(8,128)(2,1)S(1)}, u32[]{:S(2)}, u32[]{:S(2)}) async-start(bf16[8,512,128]{2,1,0:T(8,128)(2,1)} %pack.2), calls=%async_computation | async-start | bytes 2097152 | tf_op jit(solution)/shard_map/all_to_all | solution.py:630
  90.6 4.2 %copy-start.2 = (bf16[8,512,128]{2,1,0:T(8,128)(2,1)}, bf16[8,512,128]{2,1,0:T(8,128)(2,1)S(1)}, u32[]{:S(2)}) copy-start(bf16[8,512,128]{2,1,0:T(8,128)(2,1)S(1)} %all-to-all-done.gated_ref) | copy-start | bytes 3145732
  90.6 33.4 %all-to-all-start.3 = ((bf16[8,512,128]{2,1,0:T(8,128)(2,1)}), bf16[8,512,128]{2,1,0:T(8,128)(2,1)S(1)}, u32[]{:S(2)}, u32[]{:S(2)}) async-start(bf16[8,512,128]{2,1,0:T(8,128)(2,1)} %get-tuple-element.18), calls=%async_computation.3 | async-start | bytes 2097152 | tf_op jit(solution)/shard_map/all_to_all | solution.py:630
  94.7 69.0 %reduce-scatter.2.cloned.1.call-start = ((), (), s32[]{:S(2)}) async-start(), calls=%async_computation.7 | async-start | bytes 655360 | tf_op jit(solution)/shard_map/reduce_scatter | solution.py:658
  124.0 15.8 %copy-start = (bf16[8,512,128]{2,1,0:T(8,128)(2,1)}, bf16[8,512,128]{2,1,0:T(8,128)(2,1)S(1)}, u32[]{:S(2)}) copy-start(bf16[8,512,128]{2,1,0:T(8,128)(2,1)S(1)} %all-to-all-done.3.conv_ref) | copy-start | bytes 3145732
  139.8 18.9 %all-to-all-start.4 = ((bf16[8,512,128]{2,1,0:T(8,128)(2,1)}), bf16[8,512,128]{2,1,0:T(8,128)(2,1)S(1)}, u32[]{:S(2)}, u32[]{:S(2)}) async-start(bf16[8,512,128]{2,1,0:T(8,128)(2,1)} %get-tuple-element.22), calls=%async_computation.4 | async-start | bytes 2097152 | tf_op jit(solution)/shard_map/all_to_all | solution.py:630
  158.7 1.0 copy-start.1
Sparse Core Ops, SparseCore 0:
  139.9 21.6 reduce-scatter.1

commit v3 on v2

--- a/solution.py
+++ b/solution.py
@@ -630,6 +630,21 @@
     return lax.all_to_all(blocks, "ctx", split_axis=0, concat_axis=0, tiled=True)
 
 
+def gather_taps(taps):
+    groups = lax.axis_size("grp")
+    own = lax.axis_index("grp")
+    width = taps.shape[1]
+    pieces = [taps] + [
+        lax.ppermute(taps, "grp", [(g, (g + step) % groups) for g in range(groups)])
+        for step in range(1, groups)
+    ]
+    gathered = jnp.zeros((taps.shape[0], groups * width), taps.dtype)
+    for step, piece in enumerate(pieces):
+        start = lax.rem(own + (groups - step), groups) * width
+        gathered = lax.dynamic_update_slice_in_dim(gathered, piece, start, axis=1)
+    return gathered
+
+
 def per_device(signal, gate, filter_taps, skip_gain, out_cotangent):
     filters = filter_taps.shape[1] * lax.axis_size("grp")
     if (
@@ -640,7 +655,7 @@
         return per_device_general(signal, gate, filter_taps, skip_gain, out_cotangent)
     table, turns = (jnp.asarray(table) for table in dense_tables())
     gain = skip_gain[None, :]
-    all_taps = lax.all_gather(filter_taps, "grp", axis=1, tiled=True)
+    all_taps = gather_taps(filter_taps)
     taps_blocks = exchange(all_taps.reshape(ROWS, CTX, HALF).transpose(1, 0, 2))
     signal_blocks = exchange(pack_call(pack_kernel, [signal]))
     gated_blocks = exchange(pack_call(pack_gated_kernel, [gate, out_cotangent]))

time: 173 us -> 174 us (level)
  blocking collectives: 31.8 us -> 13.8 us
  waiting for transfers between devices: 28.4 us -> 37.1 us
  starting transfers between devices: 18.6 us -> 24.7 us
  local copies, waits for them, and re-layouts: 6.08 us -> 9.57 us
    all_gather x1 -> x0, blocking collectives: 18 us -> none  [per_device(): all_taps = lax.all_gather(filter_taps, 'grp', axis=1, tiled=True)]
    ppermute x0 -> x3, waiting for transfers between devices: none -> 8.75 us  [gather_taps(): lax.ppermute(taps, 'grp', [(g, (g + step) % groups) for g in range(groups)])]
    ppermute x0 -> x3, starting transfers between devices: none -> 6.11 us  [gather_taps(): lax.ppermute(taps, 'grp', [(g, (g + step) % groups) for g in range(groups)])]
    dynamic_update_slice x0 -> x4, local copies, waits for them, and re-layouts: none -> 2.65 us  [gather_taps(): gathered = lax.dynamic_update_slice_in_dim(gathered, piece, start, axis=1)]
  transfers between devices with their start and end apart: 6 -> 9, of which waited for: 3 -> 5; matrix products, arithmetic and copies ran while one was open for 1% -> 2% of each run, Pallas kernels for 42% -> 42%
where the time goes in v3:
time: 174 us; the launch traced here: 173 us
  Pallas kernels  72.5 us (42%)
  waiting for transfers between devices  37.1 us (21%)
  starting transfers between devices  24.7 us (14%)
  between operations  14.1 us (8%)
  blocking collectives  13.8 us (8%)
  local copies, waits for them, and re-layouts  9.57 us (6%)
    pallas_call x1, Pallas kernels, grad_call(): pl.pallas_call(grad_kernel, grid=(FIRST // PER_STEP,), in_specs=[whole_sp...  29.2 us
    all_to_all x5, waiting for transfers between devices, exchange(): lax.all_to_all(blocks, 'ctx', split_axis=0, concat_axis=0, tiled=True)  28.3 us
    pallas_call x1, Pallas kernels, conv_call(): pl.pallas_call(conv_kernel, grid=(FIRST // PER_STEP,), in_specs=[whole_sp...  27.1 us
    all_to_all x5, starting transfers between devices, exchange(): lax.all_to_all(blocks, 'ctx', split_axis=0, concat_axis=0, tiled=True)  18.5 us
    all_to_all x1, blocking collectives, exchange(): lax.all_to_all(blocks, 'ctx', split_axis=0, concat_axis=0, tiled=True)  13.8 us
    ppermute x3, waiting for transfers between devices, gather_taps(): lax.ppermute(taps, 'grp', [(g, (g + step) % groups) for g in range(groups)])  8.75 us
    pallas_call x2, Pallas kernels, finish_call(): pl.pallas_call(body, grid=(ROWS // PACK_ROWS,), in_specs=[packed_spec()]...  8.67 us
    pallas_call x2, Pallas kernels, pack_call(): pl.pallas_call(body, grid=(ROWS // PACK_ROWS,), in_specs=[row_spec(array....  7.51 us
  transfers between devices with their start and end apart: 9, of which 5 were waited for; matrix products, arithmetic and copies ran while one was open for 2% of the time, Pallas kernels for 42%

profile of v3, /device:TPU:0, one launch (start us, length us, event | category | flops | bytes accessed | tf_op | source)
XLA Modules:
  0.0 172.7 jit_solution(10649471374615850082)
XLA Ops:
  7.2 1.0 copy.18
  8.2 3.1 %collective-permute-start = (bf16[512,128]{0,1:T(8,128)(2,1)S(1)}, bf16[512,128]{0,1:T(8,128)(2,1)S(1)}, u32[]{:S(2)}, u32[]{:S(2)}) collective-permute-start(bf16[512,128]{0,1:T(8,128)(2,1)S(1)} %copy.18), channel_id=1, source_target_pairs={{0,1},{1,2},{2,3},{3,0},{4,5},{5,6},{6,7},{7,4},{8,9},{9,10},{10,1... | collective-permute-start | bytes 393224 | tf_op jit(solution)/shard_map/ppermute | solution.py:638
  11.3 2.1 %collective-permute-start.2 = (bf16[512,128]{0,1:T(8,128)(2,1)S(1)}, bf16[512,128]{0,1:T(8,128)(2,1)S(1)}, u32[]{:S(2)}, u32[]{:S(2)}) collective-permute-start(bf16[512,128]{0,1:T(8,128)(2,1)S(1)} %copy.18), channel_id=1, source_target_pairs={{0,3},{1,0},{2,1},{3,2},{4,7},{5,4},{6,5},{7,6},{8,11},{9,8},{10,9... | collective-permute-start | bytes 393224 | tf_op jit(solution)/shard_map/ppermute | solution.py:638
  13.3 0.9 collective-permute-start.1
  14.3 0.8 broadcast_in_dim.6
  15.1 0.7 constant_dynamic-update-slice_fusion.3
  15.8 1.8 %collective-permute-done = bf16[512,128]{0,1:T(8,128)(2,1)S(1)} collective-permute-done((bf16[512,128]{0,1:T(8,128)(2,1)S(1)}, bf16[512,128]{0,1:T(8,128)(2,1)S(1)}, u32[]{:S(2)}, u32[]{:S(2)}) %collective-permute-start) | collective-permute-done | bytes 131104 | tf_op jit(solution)/shard_map/ppermute | solution.py:638
  17.6 0.7 constant_dynamic-update-slice_fusion.2
  18.3 6.9 %collective-permute-done.1 = bf16[512,128]{0,1:T(8,128)(2,1)S(1)} collective-permute-done((bf16[512,128]{0,1:T(8,128)(2,1)S(1)}, bf16[512,128]{0,1:T(8,128)(2,1)S(1)}, u32[]{:S(2)}, u32[]{:S(2)}) %collective-permute-start.1) | collective-permute-done | bytes 131104 | tf_op jit(solution)/shard_map/ppermute | solution.py:638
  25.2 0.7 constant_dynamic-update-slice_fusion.1
  25.9 0.7 constant_dynamic-update-slice_fusion
  26.5 3.7 %all-to-all-start.2 = ((bf16[8,512,64]{1,2,0:T(8,128)(2,1)}), bf16[8,512,64]{1,2,0:T(8,128)(2,1)S(1)}, u32[]{:S(2)}, u32[]{:S(2)}) async-start(bf16[8,512,64]{1,2,0:T(8,128)(2,1)} %bitcast.1), calls=%async_computation.2 | async-start | bytes 1048576 | tf_op jit(solution)/shard_map/all_to_all | solution.py:630
  30.3 3.6 %pack.3 = bf16[8,512,128]{2,1,0:T(8,128)(2,1)} custom-call(bf16[512,1024]{1,0:T(8,128)(2,1)} %signal_ref.3), custom_call_target="tpu_custom_call" | custom-call | tf_op jit(solution)/shard_map/pack/pallas_call | solution.py:585
  33.9 6.1 %all-to-all-done.2 = bf16[8,512,64]{1,2,0:T(8,128)(2,1)S(1)} async-done(((bf16[8,512,64]{1,2,0:T(8,128)(2,1)}), bf16[8,512,64]{1,2,0:T(8,128)(2,1)S(1)}, u32[]{:S(2)}, u32[]{:S(2)}) %all-to-all-start.2) | async-done | bytes 524320 | tf_op jit(solution)/shard_map/all_to_all | solution.py:630
  40.0 3.6 %all-to-all-start.1 = ((bf16[8,512,128]{2,1,0:T(8,128)(2,1)}), bf16[8,512,128]{2,1,0:T(8,128)(2,1)S(1)}, u32[]{:S(2)}, u32[]{:S(2)}) async-start(bf16[8,512,128]{2,1,0:T(8,128)(2,1)} %pack.3), calls=%async_computation.1 | async-start | bytes 2097152 | tf_op jit(solution)/shard_map/all_to_all | solution.py:630
  43.6 3.9 %pack.2 = bf16[8,512,128]{2,1,0:T(8,128)(2,1)} custom-call(bf16[512,1024]{1,0:T(8,128)(2,1)} %gate_ref.5, bf16[512,1024]{1,0:T(8,128)(2,1)} %cotangent_ref.5), custom_call_target="tpu_custom_call" | custom-call | tf_op jit(solution)/shard_map/pack/pallas_call | solution.py:585
  47.5 11.4 %all-to-all-done.1.signal_ref = bf16[8,512,128]{2,1,0:T(8,128)(2,1)S(1)} async-done(((bf16[8,512,128]{2,1,0:T(8,128)(2,1)}), bf16[8,512,128]{2,1,0:T(8,128)(2,1)S(1)}, u32[]{:S(2)}, u32[]{:S(2)}) %all-to-all-start.1) | async-done | bytes 1048608 | tf_op jit(solution)/shard_map/all_to_all | solution.py:630
  58.9 3.6 %all-to-all-start = ((bf16[8,512,128]{2,1,0:T(8,128)(2,1)}), bf16[8,512,128]{2,1,0:T(8,128)(2,1)S(1)}, u32[]{:S(2)}, u32[]{:S(2)}) async-start(bf16[8,512,128]{2,1,0:T(8,128)(2,1)} %pack.2), calls=%async_computation | async-start | bytes 2097152 | tf_op jit(solution)/shard_map/all_to_all | solution.py:630
  62.5 1.3 copy.22.taps_ref
  63.8 27.1 %conv_part.1 = (bf16[8,512,128]{2,1,0:T(8,128)(2,1)}, bf16[16,512,128]{2,1,0:T(8,128)(2,1)}, bf16[16,512,128]{2,1,0:T(8,128)(2,1)}) custom-call(bf16[8,512,128]{2,1,0:T(8,128)(2,1)} %copy-done.3, bf16[8,512,64]{2,1,0:T(8,128)(2,1)} %copy.22.taps_ref, bf16[512,1024]{1,0:T(8,128)(2,1)} %constant.34.clone.table_ref, f32[2,512,128]{2,1,0:T(8,128)} %constant.35.clone.turns_ref), custom_call_target="tpu_custom_call" | custom-call | flops 8589934592 | bytes 62914560 | tf_op jit(solution)/shard_map/conv_part/pallas_call | solution.py:507
  90.9 4.1 %all-to-all-start.3 = ((bf16[8,512,128]{2,1,0:T(8,128)(2,1)}), bf16[8,512,128]{2,1,0:T(8,128)(2,1)S(1)}, u32[]{:S(2)}, u32[]{:S(2)}) async-start(bf16[8,512,128]{2,1,0:T(8,128)(2,1)} %get-tuple-element.18), calls=%async_computation.3 | async-start | bytes 2097152 | tf_op jit(solution)/shard_map/all_to_all | solution.py:630
  95.1 0.0 reduce-scatter.2.cloned.1.call-start
  95.1 29.2 %grad_part.1 = (bf16[8,512,128]{2,1,0:T(8,128)(2,1)}, bf16[8,512,64]{2,1,0:T(8,128)(2,1)}) custom-call(bf16[8,512,128]{2,1,0:T(8,128)(2,1)} %copy-done.2, bf16[16,512,128]{2,1,0:T(8,128)(2,1)} %get-tuple-element.14.spec_ref, bf16[16,512,128]{2,1,0:T(8,128)(2,1)} %get-tuple-element.15.filt_ref, bf16[512,1024]{1,0:T(8,128)(2,1)} %constant.34.clone.table_ref, ...), custom_call_target="tpu_custom_call" | custom-call | flops 8589934592 | bytes 62914560 | tf_op jit(solution)/shard_map/grad_part/pallas_call | solution.py:529
  124.3 1.9 %copy.23 = bf16[8,512,64]{1,2,0:T(8,128)(2,1)S(1)} copy(bf16[8,512,64]{2,1,0:T(8,128)(2,1)} %get-tuple-element.23) | data formatting | bytes 1048576 | tf_op jit(solution)/shard_map/optimization_barrier | solution.py:665
  126.3 13.8 %all_to_all.30 = bf16[8,512,64]{1,2,0:T(8,128)(2,1)} all-to-all(bf16[8,512,64]{1,2,0:T(8,128)(2,1)S(1)} %copy.23), channel_id=1, replica_groups=mesh['ctx'=8,'grp'=4] {'ctx'}, dimensions={0} | all-to-all | bytes 1048576 | tf_op jit(solution)/shard_map/all_to_all | solution.py:630
  140.1 3.6 %all-to-all-start.4 = ((bf16[8,512,128]{2,1,0:T(8,128)(2,1)}), bf16[8,512,128]{2,1,0:T(8,128)(2,1)S(1)}, u32[]{:S(2)}, u32[]{:S(2)}) async-start(bf16[8,512,128]{2,1,0:T(8,128)(2,1)} %get-tuple-element.22), calls=%async_computation.4 | async-start | bytes 2097152 | tf_op jit(solution)/shard_map/all_to_all | solution.py:630
  143.7 4.6 %finish.2 = (bf16[512,1024]{1,0:T(8,128)(2,1)}, bf16[512,1024]{1,0:T(8,128)(2,1)}) custom-call(bf16[8,512,128]{2,1,0:T(8,128)(2,1)} %copy-done, bf16[512,1024]{1,0:T(8,128)(2,1)} %signal_ref.3, bf16[512,1024]{1,0:T(8,128)(2,1)} %gate_ref.5, bf16[512,1024]{1,0:T(8,128)(2,1)} %cotangent_ref.5, f32[1,1024]{1,0:T(1,128)} %bitcast.8), custom_call_target="tpu_custom_call" | custom-call | tf_op jit(solution)/shard_map/finish/pallas_call | solution.py:617
  148.3 10.7 %all-to-all-done.4.grad_ref = bf16[8,512,128]{2,1,0:T(8,128)(2,1)S(1)} async-done(((bf16[8,512,128]{2,1,0:T(8,128)(2,1)}), bf16[8,512,128]{2,1,0:T(8,128)(2,1)S(1)}, u32[]{:S(2)}, u32[]{:S(2)}) %all-to-all-start.4) | async-done | bytes 1048608 | tf_op jit(solution)/shard_map/all_to_all | solution.py:630
  159.0 1.0 copy-done.1
  160.0 4.1 %finish.3 = bf16[512,1024]{1,0:T(8,128)(2,1)} custom-call(bf16[8,512,128]{2,1,0:T(8,128)(2,1)} %copy-done.1, bf16[512,1024]{1,0:T(8,128)(2,1)} %gate_ref.5, bf16[512,1024]{1,0:T(8,128)(2,1)} %cotangent_ref.5, f32[1,1024]{1,0:T(1,128)} %bitcast.9), custom_call_target="tpu_custom_call" | custom-call | tf_op jit(solution)/shard_map/finish/pallas_call | solution.py:617
  164.1 0.9 convert_multiply_fusion
  165.0 0.8 copy.24
  (12 shorter events, 0.0 us)
Async XLA Ops:
  8.2 9.4 %collective-permute-start = (bf16[512,128]{0,1:T(8,128)(2,1)S(1)}, bf16[512,128]{0,1:T(8,128)(2,1)S(1)}, u32[]{:S(2)}, u32[]{:S(2)}) collective-permute-start(bf16[512,128]{0,1:T(8,128)(2,1)S(1)} %copy.18), channel_id=1, source_target_pairs={{0,1},{1,2},{2,3},{3,0},{4,5},{5,6},{6,7},{7,4},{8,9},{9,10},{10,1... | collective-permute-start | bytes 393224 | tf_op jit(solution)/shard_map/ppermute | solution.py:638
  11.3 14.6 %collective-permute-start.2 = (bf16[512,128]{0,1:T(8,128)(2,1)S(1)}, bf16[512,128]{0,1:T(8,128)(2,1)S(1)}, u32[]{:S(2)}, u32[]{:S(2)}) collective-permute-start(bf16[512,128]{0,1:T(8,128)(2,1)S(1)} %copy.18), channel_id=1, source_target_pairs={{0,3},{1,0},{2,1},{3,2},{4,7},{5,4},{6,5},{7,6},{8,11},{9,8},{10,9... | collective-permute-start | bytes 393224 | tf_op jit(solution)/shard_map/ppermute | solution.py:638
  13.3 11.9 %collective-permute-start.1 = (bf16[512,128]{0,1:T(8,128)(2,1)S(1)}, bf16[512,128]{0,1:T(8,128)(2,1)S(1)}, u32[]{:S(2)}, u32[]{:S(2)}) collective-permute-start(bf16[512,128]{0,1:T(8,128)(2,1)S(1)} %copy.18), channel_id=1, source_target_pairs={{0,2},{1,3},{2,0},{3,1},{4,6},{5,7},{6,4},{7,5},{8,10},{9,11},{10,... | collective-permute-start | bytes 393224 | tf_op jit(solution)/shard_map/ppermute | solution.py:638
  26.5 13.5 %all-to-all-start.2 = ((bf16[8,512,64]{1,2,0:T(8,128)(2,1)}), bf16[8,512,64]{1,2,0:T(8,128)(2,1)S(1)}, u32[]{:S(2)}, u32[]{:S(2)}) async-start(bf16[8,512,64]{1,2,0:T(8,128)(2,1)} %bitcast.1), calls=%async_computation.2 | async-start | bytes 1048576 | tf_op jit(solution)/shard_map/all_to_all | solution.py:630
  40.0 18.9 %all-to-all-start.1 = ((bf16[8,512,128]{2,1,0:T(8,128)(2,1)}), bf16[8,512,128]{2,1,0:T(8,128)(2,1)S(1)}, u32[]{:S(2)}, u32[]{:S(2)}) async-start(bf16[8,512,128]{2,1,0:T(8,128)(2,1)} %pack.3), calls=%async_computation.1 | async-start | bytes 2097152 | tf_op jit(solution)/shard_map/all_to_all | solution.py:630
  58.9 4.9 %copy-start.3 = (bf16[8,512,128]{2,1,0:T(8,128)(2,1)}, bf16[8,512,128]{2,1,0:T(8,128)(2,1)S(1)}, u32[]{:S(2)}) copy-start(bf16[8,512,128]{2,1,0:T(8,128)(2,1)S(1)} %all-to-all-done.1.signal_ref) | copy-start | bytes 3145732
  58.9 32.0 %all-to-all-start = ((bf16[8,512,128]{2,1,0:T(8,128)(2,1)}), bf16[8,512,128]{2,1,0:T(8,128)(2,1)S(1)}, u32[]{:S(2)}, u32[]{:S(2)}) async-start(bf16[8,512,128]{2,1,0:T(8,128)(2,1)} %pack.2), calls=%async_computation | async-start | bytes 2097152 | tf_op jit(solution)/shard_map/all_to_all | solution.py:630
  90.9 4.2 %copy-start.2 = (bf16[8,512,128]{2,1,0:T(8,128)(2,1)}, bf16[8,512,128]{2,1,0:T(8,128)(2,1)S(1)}, u32[]{:S(2)}) copy-start(bf16[8,512,128]{2,1,0:T(8,128)(2,1)S(1)} %all-to-all-done.gated_ref) | copy-start | bytes 3145732
  90.9 33.4 %all-to-all-start.3 = ((bf16[8,512,128]{2,1,0:T(8,128)(2,1)}), bf16[8,512,128]{2,1,0:T(8,128)(2,1)S(1)}, u32[]{:S(2)}, u32[]{:S(2)}) async-start(bf16[8,512,128]{2,1,0:T(8,128)(2,1)} %get-tuple-element.18), calls=%async_computation.3 | async-start | bytes 2097152 | tf_op jit(solution)/shard_map/all_to_all | solution.py:630
  95.1 69.0 %reduce-scatter.2.cloned.1.call-start = ((), (), s32[]{:S(2)}) async-start(), calls=%async_computation.7 | async-start | bytes 655360 | tf_op jit(solution)/shard_map/reduce_scatter | solution.py:673
  124.3 15.8 %copy-start = (bf16[8,512,128]{2,1,0:T(8,128)(2,1)}, bf16[8,512,128]{2,1,0:T(8,128)(2,1)S(1)}, u32[]{:S(2)}) copy-start(bf16[8,512,128]{2,1,0:T(8,128)(2,1)S(1)} %all-to-all-done.3.conv_ref) | copy-start | bytes 3145732
  140.1 18.9 %all-to-all-start.4 = ((bf16[8,512,128]{2,1,0:T(8,128)(2,1)}), bf16[8,512,128]{2,1,0:T(8,128)(2,1)S(1)}, u32[]{:S(2)}, u32[]{:S(2)}) async-start(bf16[8,512,128]{2,1,0:T(8,128)(2,1)} %get-tuple-element.22), calls=%async_computation.4 | async-start | bytes 2097152 | tf_op jit(solution)/shard_map/all_to_all | solution.py:630
  159.0 1.0 copy-start.1
Sparse Core Ops, SparseCore 0:
  140.2 19.0 reduce-scatter.1

commit v4 on v3

--- a/solution.py
+++ b/solution.py
@@ -630,7 +630,7 @@
     return lax.all_to_all(blocks, "ctx", split_axis=0, concat_axis=0, tiled=True)
 
 
-def gather_taps(taps):
+def gather_taps(taps, after):
     groups = lax.axis_size("grp")
     own = lax.axis_index("grp")
     width = taps.shape[1]
@@ -638,11 +638,12 @@
         lax.ppermute(taps, "grp", [(g, (g + step) % groups) for g in range(groups)])
         for step in range(1, groups)
     ]
+    pieces, after = lax.optimization_barrier((pieces, after))
     gathered = jnp.zeros((taps.shape[0], groups * width), taps.dtype)
     for step, piece in enumerate(pieces):
         start = lax.rem(own + (groups - step), groups) * width
         gathered = lax.dynamic_update_slice_in_dim(gathered, piece, start, axis=1)
-    return gathered
+    return gathered, after
 
 
 def per_device(signal, gate, filter_taps, skip_gain, out_cotangent):
@@ -655,9 +656,9 @@
         return per_device_general(signal, gate, filter_taps, skip_gain, out_cotangent)
     table, turns = (jnp.asarray(table) for table in dense_tables())
     gain = skip_gain[None, :]
-    all_taps = gather_taps(filter_taps)
+    signal_blocks = exchange(pack_call(pack_kernel, [signal]))
+    all_taps, signal_blocks = gather_taps(filter_taps, signal_blocks)
     taps_blocks = exchange(all_taps.reshape(ROWS, CTX, HALF).transpose(1, 0, 2))
-    signal_blocks = exchange(pack_call(pack_kernel, [signal]))
     gated_blocks = exchange(pack_call(pack_gated_kernel, [gate, out_cotangent]))
     conv, spec, filt = conv_call(signal_blocks, taps_blocks, table, turns)
     conv_back = exchange(conv)

time: 174 us -> 164 us (0.943)
  waiting for transfers between devices: 37.1 us -> 27.8 us
    all_to_all x5, waiting for transfers between devices: 28.3 us -> 16.6 us  [exchange(): lax.all_to_all(blocks, 'ctx', split_axis=0, concat_axis=0, tiled=True)]
    ppermute x3, waiting for transfers between devices: 8.75 us -> 11.1 us  [gather_taps(): lax.ppermute(taps, 'grp', [(g, (g + step) % groups) for g in range(groups)])]
  transfers between devices with their start and end apart: 9 -> 9, of which waited for: 5 -> 4; matrix products, arithmetic and copies ran while one was open for 2% -> 1% of each run, Pallas kernels for 42% -> 42%
where the time goes in v4:
time: 164 us; the launch traced here: 163 us
  Pallas kernels  72.5 us (44%)
  waiting for transfers between devices  27.8 us (17%)
  starting transfers between devices  24.9 us (15%)
  between operations  14.1 us (9%)
  blocking collectives  13.8 us (8%)
  local copies, waits for them, and re-layouts  8.92 us (5%)
    pallas_call x1, Pallas kernels, grad_call(): pl.pallas_call(grad_kernel, grid=(FIRST // PER_STEP,), in_specs=[whole_sp...  29.2 us
    pallas_call x1, Pallas kernels, conv_call(): pl.pallas_call(conv_kernel, grid=(FIRST // PER_STEP,), in_specs=[whole_sp...  27.1 us
    all_to_all x5, starting transfers between devices, exchange(): lax.all_to_all(blocks, 'ctx', split_axis=0, concat_axis=0, tiled=True)  20.2 us
    all_to_all x5, waiting for transfers between devices, exchange(): lax.all_to_all(blocks, 'ctx', split_axis=0, concat_axis=0, tiled=True)  16.6 us
    all_to_all x1, blocking collectives, exchange(): lax.all_to_all(blocks, 'ctx', split_axis=0, concat_axis=0, tiled=True)  13.8 us
    ppermute x3, waiting for transfers between devices, gather_taps(): lax.ppermute(taps, 'grp', [(g, (g + step) % groups) for g in range(groups)])  11.1 us
    pallas_call x2, Pallas kernels, finish_call(): pl.pallas_call(body, grid=(ROWS // PACK_ROWS,), in_specs=[packed_spec()]...  8.74 us
    pallas_call x2, Pallas kernels, pack_call(): pl.pallas_call(body, grid=(ROWS // PACK_ROWS,), in_specs=[row_spec(array....  7.45 us
  transfers between devices with their start and end apart: 9, of which 4 were waited for; matrix products, arithmetic and copies ran while one was open for 1% of the time, Pallas kernels for 42%

profile of v4, /device:TPU:0, one launch (start us, length us, event | category | flops | bytes accessed | tf_op | source)
XLA Modules:
  0.0 163.0 jit_solution(1080836136328276589)
XLA Ops:
  7.2 3.6 %pack.3 = bf16[8,512,128]{2,1,0:T(8,128)(2,1)} custom-call(bf16[512,1024]{1,0:T(8,128)(2,1)} %signal_ref.3), custom_call_target="tpu_custom_call" | custom-call | tf_op jit(solution)/shard_map/pack/pallas_call | solution.py:585
  10.8 5.2 %all-to-all-start.1 = ((bf16[8,512,128]{2,1,0:T(8,128)(2,1)}), bf16[8,512,128]{2,1,0:T(8,128)(2,1)S(1)}, u32[]{:S(2)}, u32[]{:S(2)}) async-start(bf16[8,512,128]{2,1,0:T(8,128)(2,1)} %pack.3), calls=%async_computation.1 | async-start | bytes 2097152 | tf_op jit(solution)/shard_map/all_to_all | solution.py:630
  16.0 0.1 copy.18
  16.1 3.7 %collective-permute-start.2 = (bf16[512,128]{0,1:T(8,128)(2,1)S(1)}, bf16[512,128]{0,1:T(8,128)(2,1)S(1)}, u32[]{:S(2)}, u32[]{:S(2)}) collective-permute-start(bf16[512,128]{0,1:T(8,128)(2,1)S(1)} %copy.18), channel_id=1, source_target_pairs={{0,3},{1,0},{2,1},{3,2},{4,7},{5,4},{6,5},{7,6},{8,11},{9,8},{10,9... | collective-permute-start | bytes 393224 | tf_op jit(solution)/shard_map/ppermute | solution.py:638
  19.8 1.0 collective-permute-start
  20.8 2.9 %collective-permute-done.2 = bf16[512,128]{0,1:T(8,128)(2,1)S(1)} collective-permute-done((bf16[512,128]{0,1:T(8,128)(2,1)S(1)}, bf16[512,128]{0,1:T(8,128)(2,1)S(1)}, u32[]{:S(2)}, u32[]{:S(2)}) %collective-permute-start.2) | collective-permute-done | bytes 131104 | tf_op jit(solution)/shard_map/ppermute | solution.py:638
  23.7 8.2 %collective-permute-done.1 = bf16[512,128]{0,1:T(8,128)(2,1)S(1)} collective-permute-done((bf16[512,128]{0,1:T(8,128)(2,1)S(1)}, bf16[512,128]{0,1:T(8,128)(2,1)S(1)}, u32[]{:S(2)}, u32[]{:S(2)}) %collective-permute-start.1) | collective-permute-done | bytes 131104 | tf_op jit(solution)/shard_map/ppermute | solution.py:638
  31.9 0.1 copy.21
  32.0 1.0 broadcast_in_dim.6
  33.0 0.7 constant_dynamic-update-slice_fusion.3
  33.7 0.7 constant_dynamic-update-slice_fusion.2
  34.3 0.7 constant_dynamic-update-slice_fusion.1
  35.0 0.7 constant_dynamic-update-slice_fusion
  35.7 3.8 %all-to-all-start.2 = ((bf16[8,512,64]{1,2,0:T(8,128)(2,1)}), bf16[8,512,64]{1,2,0:T(8,128)(2,1)S(1)}, u32[]{:S(2)}, u32[]{:S(2)}) async-start(bf16[8,512,64]{1,2,0:T(8,128)(2,1)} %bitcast.1), calls=%async_computation.2 | async-start | bytes 1048576 | tf_op jit(solution)/shard_map/all_to_all | solution.py:630
  39.4 3.8 %pack.2 = bf16[8,512,128]{2,1,0:T(8,128)(2,1)} custom-call(bf16[512,1024]{1,0:T(8,128)(2,1)} %gate_ref.5, bf16[512,1024]{1,0:T(8,128)(2,1)} %cotangent_ref.5), custom_call_target="tpu_custom_call" | custom-call | tf_op jit(solution)/shard_map/pack/pallas_call | solution.py:585
  43.2 5.9 %all-to-all-done.2 = bf16[8,512,64]{1,2,0:T(8,128)(2,1)S(1)} async-done(((bf16[8,512,64]{1,2,0:T(8,128)(2,1)}), bf16[8,512,64]{1,2,0:T(8,128)(2,1)S(1)}, u32[]{:S(2)}, u32[]{:S(2)}) %all-to-all-start.2) | async-done | bytes 524320 | tf_op jit(solution)/shard_map/all_to_all | solution.py:630
  49.2 3.6 %all-to-all-start = ((bf16[8,512,128]{2,1,0:T(8,128)(2,1)}), bf16[8,512,128]{2,1,0:T(8,128)(2,1)S(1)}, u32[]{:S(2)}, u32[]{:S(2)}) async-start(bf16[8,512,128]{2,1,0:T(8,128)(2,1)} %pack.2), calls=%async_computation | async-start | bytes 2097152 | tf_op jit(solution)/shard_map/all_to_all | solution.py:630
  52.7 1.3 copy.22.taps_ref
  54.0 27.1 %conv_part.1 = (bf16[8,512,128]{2,1,0:T(8,128)(2,1)}, bf16[16,512,128]{2,1,0:T(8,128)(2,1)}, bf16[16,512,128]{2,1,0:T(8,128)(2,1)}) custom-call(bf16[8,512,128]{2,1,0:T(8,128)(2,1)} %copy-done.2, bf16[8,512,64]{2,1,0:T(8,128)(2,1)} %copy.22.taps_ref, bf16[512,1024]{1,0:T(8,128)(2,1)} %constant.34.clone.table_ref, f32[2,512,128]{2,1,0:T(8,128)} %constant.35.clone.turns_ref), custom_call_target="tpu_custom_call" | custom-call | flops 8589934592 | bytes 62914560 | tf_op jit(solution)/shard_map/conv_part/pallas_call | solution.py:507
  81.1 4.1 %all-to-all-start.3 = ((bf16[8,512,128]{2,1,0:T(8,128)(2,1)}), bf16[8,512,128]{2,1,0:T(8,128)(2,1)S(1)}, u32[]{:S(2)}, u32[]{:S(2)}) async-start(bf16[8,512,128]{2,1,0:T(8,128)(2,1)} %get-tuple-element.28), calls=%async_computation.3 | async-start | bytes 2097152 | tf_op jit(solution)/shard_map/all_to_all | solution.py:630
  85.3 0.0 reduce-scatter.2.cloned.1.call-start
  85.3 29.2 %grad_part.1 = (bf16[8,512,128]{2,1,0:T(8,128)(2,1)}, bf16[8,512,64]{2,1,0:T(8,128)(2,1)}) custom-call(bf16[8,512,128]{2,1,0:T(8,128)(2,1)} %copy-done.3, bf16[16,512,128]{2,1,0:T(8,128)(2,1)} %get-tuple-element.24.spec_ref, bf16[16,512,128]{2,1,0:T(8,128)(2,1)} %get-tuple-element.25.filt_ref, bf16[512,1024]{1,0:T(8,128)(2,1)} %constant.34.clone.table_ref, ...), custom_call_target="tpu_custom_call" | custom-call | flops 8589934592 | bytes 62914560 | tf_op jit(solution)/shard_map/grad_part/pallas_call | solution.py:529
  114.6 1.9 %copy.23 = bf16[8,512,64]{1,2,0:T(8,128)(2,1)S(1)} copy(bf16[8,512,64]{2,1,0:T(8,128)(2,1)} %get-tuple-element.33) | data formatting | bytes 1048576 | tf_op jit(solution)/shard_map/optimization_barrier | solution.py:666
  116.5 13.8 %all_to_all.30 = bf16[8,512,64]{1,2,0:T(8,128)(2,1)} all-to-all(bf16[8,512,64]{1,2,0:T(8,128)(2,1)S(1)} %copy.23), channel_id=1, replica_groups=mesh['ctx'=8,'grp'=4] {'ctx'}, dimensions={0} | all-to-all | bytes 1048576 | tf_op jit(solution)/shard_map/all_to_all | solution.py:630
  130.3 0.0 reduce-scatter.2.cloned.1.call-update
  130.3 3.6 %all-to-all-start.4 = ((bf16[8,512,128]{2,1,0:T(8,128)(2,1)}), bf16[8,512,128]{2,1,0:T(8,128)(2,1)S(1)}, u32[]{:S(2)}, u32[]{:S(2)}) async-start(bf16[8,512,128]{2,1,0:T(8,128)(2,1)} %get-tuple-element.32), calls=%async_computation.4 | async-start | bytes 2097152 | tf_op jit(solution)/shard_map/all_to_all | solution.py:630
  133.9 4.6 %finish.2 = (bf16[512,1024]{1,0:T(8,128)(2,1)}, bf16[512,1024]{1,0:T(8,128)(2,1)}) custom-call(bf16[8,512,128]{2,1,0:T(8,128)(2,1)} %copy-done, bf16[512,1024]{1,0:T(8,128)(2,1)} %signal_ref.3, bf16[512,1024]{1,0:T(8,128)(2,1)} %gate_ref.5, bf16[512,1024]{1,0:T(8,128)(2,1)} %cotangent_ref.5, f32[1,1024]{1,0:T(1,128)} %bitcast.8), custom_call_target="tpu_custom_call" | custom-call | tf_op jit(solution)/shard_map/finish/pallas_call | solution.py:617
  138.6 10.7 %all-to-all-done.4.grad_ref = bf16[8,512,128]{2,1,0:T(8,128)(2,1)S(1)} async-done(((bf16[8,512,128]{2,1,0:T(8,128)(2,1)}), bf16[8,512,128]{2,1,0:T(8,128)(2,1)S(1)}, u32[]{:S(2)}, u32[]{:S(2)}) %all-to-all-start.4) | async-done | bytes 1048608 | tf_op jit(solution)/shard_map/all_to_all | solution.py:630
  149.3 1.0 copy-done.1
  150.2 4.1 %finish.3 = bf16[512,1024]{1,0:T(8,128)(2,1)} custom-call(bf16[8,512,128]{2,1,0:T(8,128)(2,1)} %copy-done.1, bf16[512,1024]{1,0:T(8,128)(2,1)} %gate_ref.5, bf16[512,1024]{1,0:T(8,128)(2,1)} %cotangent_ref.5, f32[1,1024]{1,0:T(1,128)} %bitcast.9), custom_call_target="tpu_custom_call" | custom-call | tf_op jit(solution)/shard_map/finish/pallas_call | solution.py:617
  154.3 0.9 convert_multiply_fusion
  155.3 0.8 copy.24
  (15 shorter events, 0.0 us)
Async XLA Ops:
  7.2 8.8 %copy-start.4 = (bf16[512,128]{1,0:T(8,128)(2,1)S(1)}, bf16[512,128]{1,0:T(8,128)(2,1)}, u32[]{:S(2)}) copy-start(bf16[512,128]{1,0:T(8,128)(2,1)} %param.9) | copy-start | bytes 393220
  10.8 21.1 %all-to-all-start.1 = ((bf16[8,512,128]{2,1,0:T(8,128)(2,1)}), bf16[8,512,128]{2,1,0:T(8,128)(2,1)S(1)}, u32[]{:S(2)}, u32[]{:S(2)}) async-start(bf16[8,512,128]{2,1,0:T(8,128)(2,1)} %pack.3), calls=%async_computation.1 | async-start | bytes 2097152 | tf_op jit(solution)/shard_map/all_to_all | solution.py:630
  16.1 7.6 %collective-permute-start.2 = (bf16[512,128]{0,1:T(8,128)(2,1)S(1)}, bf16[512,128]{0,1:T(8,128)(2,1)S(1)}, u32[]{:S(2)}, u32[]{:S(2)}) collective-permute-start(bf16[512,128]{0,1:T(8,128)(2,1)S(1)} %copy.18), channel_id=1, source_target_pairs={{0,3},{1,0},{2,1},{3,2},{4,7},{5,4},{6,5},{7,6},{8,11},{9,8},{10,9... | collective-permute-start | bytes 393224 | tf_op jit(solution)/shard_map/ppermute | solution.py:638
  19.8 12.1 %collective-permute-start.1 = (bf16[512,128]{0,1:T(8,128)(2,1)S(1)}, bf16[512,128]{0,1:T(8,128)(2,1)S(1)}, u32[]{:S(2)}, u32[]{:S(2)}) collective-permute-start(bf16[512,128]{0,1:T(8,128)(2,1)S(1)} %copy.18), channel_id=1, source_target_pairs={{0,2},{1,3},{2,0},{3,1},{4,6},{5,7},{6,4},{7,5},{8,10},{9,11},{10,... | collective-permute-start | bytes 393224 | tf_op jit(solution)/shard_map/ppermute | solution.py:638
  19.8 12.1 %collective-permute-start = (bf16[512,128]{0,1:T(8,128)(2,1)S(1)}, bf16[512,128]{0,1:T(8,128)(2,1)S(1)}, u32[]{:S(2)}, u32[]{:S(2)}) collective-permute-start(bf16[512,128]{0,1:T(8,128)(2,1)S(1)} %copy.18), channel_id=1, source_target_pairs={{0,1},{1,2},{2,3},{3,0},{4,5},{5,6},{6,7},{7,4},{8,9},{9,10},{10,1... | collective-permute-start | bytes 393224 | tf_op jit(solution)/shard_map/ppermute | solution.py:638
  31.9 11.3 %copy-start.2 = (bf16[8,512,128]{2,1,0:T(8,128)(2,1)}, bf16[8,512,128]{2,1,0:T(8,128)(2,1)S(1)}, u32[]{:S(2)}) copy-start(bf16[8,512,128]{2,1,0:T(8,128)(2,1)S(1)} %all-to-all-done.1.signal_ref) | copy-start | bytes 3145732
  35.7 13.5 %all-to-all-start.2 = ((bf16[8,512,64]{1,2,0:T(8,128)(2,1)}), bf16[8,512,64]{1,2,0:T(8,128)(2,1)S(1)}, u32[]{:S(2)}, u32[]{:S(2)}) async-start(bf16[8,512,64]{1,2,0:T(8,128)(2,1)} %bitcast.1), calls=%async_computation.2 | async-start | bytes 1048576 | tf_op jit(solution)/shard_map/all_to_all | solution.py:630
  49.2 32.0 %all-to-all-start = ((bf16[8,512,128]{2,1,0:T(8,128)(2,1)}), bf16[8,512,128]{2,1,0:T(8,128)(2,1)S(1)}, u32[]{:S(2)}, u32[]{:S(2)}) async-start(bf16[8,512,128]{2,1,0:T(8,128)(2,1)} %pack.2), calls=%async_computation | async-start | bytes 2097152 | tf_op jit(solution)/shard_map/all_to_all | solution.py:630
  81.1 4.2 %copy-start.3 = (bf16[8,512,128]{2,1,0:T(8,128)(2,1)}, bf16[8,512,128]{2,1,0:T(8,128)(2,1)S(1)}, u32[]{:S(2)}) copy-start(bf16[8,512,128]{2,1,0:T(8,128)(2,1)S(1)} %all-to-all-done.gated_ref) | copy-start | bytes 3145732
  81.1 33.4 %all-to-all-start.3 = ((bf16[8,512,128]{2,1,0:T(8,128)(2,1)}), bf16[8,512,128]{2,1,0:T(8,128)(2,1)S(1)}, u32[]{:S(2)}, u32[]{:S(2)}) async-start(bf16[8,512,128]{2,1,0:T(8,128)(2,1)} %get-tuple-element.28), calls=%async_computation.3 | async-start | bytes 2097152 | tf_op jit(solution)/shard_map/all_to_all | solution.py:630
  85.3 69.1 %reduce-scatter.2.cloned.1.call-start = ((), (), s32[]{:S(2)}) async-start(), calls=%async_computation.7 | async-start | bytes 655360 | tf_op jit(solution)/shard_map/reduce_scatter | solution.py:674
  114.6 15.8 %copy-start = (bf16[8,512,128]{2,1,0:T(8,128)(2,1)}, bf16[8,512,128]{2,1,0:T(8,128)(2,1)S(1)}, u32[]{:S(2)}) copy-start(bf16[8,512,128]{2,1,0:T(8,128)(2,1)S(1)} %all-to-all-done.3.conv_ref) | copy-start | bytes 3145732
  130.3 18.9 %all-to-all-start.4 = ((bf16[8,512,128]{2,1,0:T(8,128)(2,1)}), bf16[8,512,128]{2,1,0:T(8,128)(2,1)S(1)}, u32[]{:S(2)}, u32[]{:S(2)}) async-start(bf16[8,512,128]{2,1,0:T(8,128)(2,1)} %get-tuple-element.32), calls=%async_computation.4 | async-start | bytes 2097152 | tf_op jit(solution)/shard_map/all_to_all | solution.py:630
  149.3 1.0 copy-start.1
Sparse Core Ops, SparseCore 0:
  130.5 20.1 reduce-scatter.1
